TPU v7x, 32 devices: a whole 2x2x4 slice. The times are simulated.
32 devices in a mesh: dev: 32 (over z, y, x, core).
Axes of the slice: x: 2, y: 2, z: 4, core: 2. Of those that a mesh axis runs over, the one named last changes fastest.
Arguments:
- embeddings: bfloat16 [64, 128, 1280], P('dev')
- lengths: int32 [64], replicated, may hold values from 16 to 128, as said below
- pairs: int32 [32, 2], replicated, may hold values from 0 to 63, as said below
- labels: int32 [32], P('dev'), may hold values 0 or 1
- w_query: bfloat16 [1280, 1280], replicated, may hold values from -0.15625 to 0.15625
- w_key: bfloat16 [1280, 1280], replicated, may hold values from -0.15625 to 0.15625
- w_value: bfloat16 [1280, 1280], replicated, may hold values from -0.15625 to 0.15625
- w_out: bfloat16 [1280, 1280], replicated, may hold values from -0.15625 to 0.15625
- w_class: float32 [1280], replicated, may hold values from -4 to 4
Outputs:
- d_embeddings: float32 [64, 128, 1280], P('dev')
- d_weights: float32 [1280, 4, 1280], P('dev')
Inputs may be any that keep to these rules, and one draw needn't show every extreme that they name: `pairs`: the two ids of a pair differ. `lengths`: some chain has exactly 128 residues.
All inputs are finite; a program needn't handle non-finite values. No bound on the sum of `labels` on one device may be relied on, other than what follows from the above.
Results may differ from a plain program's by a relative error of at most 0.013.
Values may be sent and summed in bfloat16 or wider, within the bound.
A program may use at most 192 MiB of HBM per device.

v0:
```python
import jax
import jax.numpy as jnp
from jax import lax
from jax.sharding import PartitionSpec as P

HEADS = 16


def attend(query, keys, values, key_lens):
    npair, sides, length, width = query.shape
    head_dim = width // HEADS
    qh = query.reshape(npair, sides, length, HEADS, head_dim).astype(jnp.float32)
    kh = keys.reshape(npair, sides, length, HEADS, head_dim).astype(jnp.float32)
    vh = values.reshape(npair, sides, length, HEADS, head_dim).astype(jnp.float32)
    scores = jnp.einsum("psqhd,pskhd->pshqk", qh, kh) * head_dim ** (-0.5)
    slots = jnp.arange(length, dtype=jnp.int32)
    key_valid = slots[None, None, None, None, :] < key_lens[:, :, None, None, None]
    scores = jnp.where(key_valid, scores, -1000000000.0)
    scores = scores - jnp.max(scores, axis=-1, keepdims=True)
    expo = jnp.exp(scores)
    probs = (expo / jnp.sum(expo, axis=-1, keepdims=True)).astype(jnp.bfloat16)
    context = jnp.einsum("pshqk,pskhd->psqhd", probs.astype(jnp.float32), vh)
    return context.reshape(npair, sides, length, width).astype(jnp.bfloat16)


def forward_backward(chains, chain_lens, pair_labels, w_query, w_key, w_value, w_out, w_class):
    npair, sides, length, width = chains.shape
    flat_x = chains.reshape(-1, width)
    query = (
        jnp.dot(flat_x, w_query, preferred_element_type=jnp.float32)
        .astype(jnp.bfloat16)
        .reshape(chains.shape)
    )
    keys = (
        jnp.dot(flat_x, w_key, preferred_element_type=jnp.float32)
        .astype(jnp.bfloat16)
        .reshape(chains.shape)
    )
    values = (
        jnp.dot(flat_x, w_value, preferred_element_type=jnp.float32)
        .astype(jnp.bfloat16)
        .reshape(chains.shape)
    )
    other_lens = chain_lens[:, ::-1]

    def attention(q_in, k_in, v_in):
        return attend(q_in, k_in, v_in, other_lens)

    context, attention_back = jax.vjp(attention, query, keys[:, ::-1], values[:, ::-1])
    flat_ctx = context.reshape(-1, width)
    outputs = jnp.dot(flat_ctx, w_out, preferred_element_type=jnp.float32).reshape(chains.shape)
    slots = jnp.arange(length, dtype=jnp.int32)
    valid = (slots[None, None, :] < chain_lens[:, :, None]).astype(jnp.float32)
    lens_float = chain_lens.astype(jnp.float32)
    mixed = chains.astype(jnp.float32) + outputs
    pooled = jnp.sum(mixed * valid[..., None], axis=2) / lens_float[..., None]
    logits = jnp.sum(w_class[None, :] * pooled[:, 0] * pooled[:, 1], axis=-1)
    slope = jax.nn.sigmoid(logits) - pair_labels.astype(jnp.float32)
    d_pooled = slope[:, None, None] * w_class[None, None, :] * pooled[:, ::-1]
    d_mixed = valid[..., None] * (d_pooled / lens_float[..., None])[:, :, None, :]
    d_out = d_mixed.astype(jnp.bfloat16).reshape(-1, width)
    d_ctx = lax.dot_general(
        d_out, w_out, (((1,), (1,)), ((), ())), preferred_element_type=jnp.float32
    )
    d_ctx = d_ctx.astype(jnp.bfloat16).reshape(chains.shape)
    d_query, d_keys_other, d_values_other = attention_back(d_ctx)
    d_keys = d_keys_other[:, ::-1]
    d_values = d_values_other[:, ::-1]
    grads_three = jnp.concatenate(
        [d_query.reshape(-1, width), d_keys.reshape(-1, width), d_values.reshape(-1, width)], axis=1
    )
    stacked = jnp.concatenate([w_query, w_key, w_value], axis=1)
    back_in = lax.dot_general(
        grads_three, stacked, (((1,), (1,)), ((), ())), preferred_element_type=jnp.float32
    )
    d_input = d_mixed + back_in.reshape(chains.shape)
    return (d_input, flat_x, grads_three, flat_ctx, d_out)


def weight_grads(flat_x, grads_three, flat_ctx, d_out):
    upper = lax.dot_general(
        flat_x, grads_three, (((0,), (0,)), ((), ())), preferred_element_type=jnp.float32
    )
    lower = lax.dot_general(
        flat_ctx, d_out, (((0,), (0,)), ((), ())), preferred_element_type=jnp.float32
    )
    joined = jnp.concatenate([upper, lower], axis=1)
    return joined.reshape(flat_x.shape[1], 4, d_out.shape[1])


def shards(embeddings, lengths, pairs, labels, w_query, w_key, w_value, w_out, w_class):
    pair_dev = labels.shape[0]
    length = embeddings.shape[1]
    width = embeddings.shape[2]
    chain_total = lengths.shape[0]
    spread = lax.all_to_all(embeddings, "dev", split_axis=1, concat_axis=0, tiled=True)
    slot_ids = pairs.reshape(-1)
    picked = jnp.take(spread, slot_ids, axis=0)
    gathered = lax.all_to_all(picked, "dev", split_axis=0, concat_axis=1, tiled=True)
    chains = gathered.reshape(pair_dev, 2, length, width)
    first_pair = lax.axis_index("dev") * pair_dev
    my_pairs = lax.dynamic_slice_in_dim(pairs, first_pair, pair_dev, 0)
    chain_lens = jnp.take(lengths, my_pairs, axis=0)
    d_input, flat_x, grads_three, flat_ctx, d_out = forward_backward(
        chains, chain_lens, labels, w_query, w_key, w_value, w_out, w_class
    )
    d_weights = lax.psum_scatter(
        weight_grads(flat_x, grads_three, flat_ctx, d_out), "dev", scatter_dimension=0, tiled=True
    )
    slot_grads = d_input.reshape(2 * pair_dev, length, width)
    by_rows = lax.all_to_all(slot_grads, "dev", split_axis=1, concat_axis=0, tiled=True)
    row_block = by_rows.shape[1]
    chain_index = jnp.arange(chain_total, dtype=jnp.int32)
    selector = (chain_index[:, None] == slot_ids[None, :]).astype(jnp.float32)
    summed = jnp.dot(
        selector,
        by_rows.reshape(slot_ids.shape[0], row_block * width),
        precision=lax.Precision.HIGHEST,
        preferred_element_type=jnp.float32,
    )
    summed = summed.reshape(chain_total, row_block, width)
    d_embeddings = lax.all_to_all(summed, "dev", split_axis=0, concat_axis=1, tiled=True)
    return (d_embeddings, d_weights)


def solution(mesh):
    placed = (P("dev", None, None), P(), P(), P("dev"), P(), P(), P(), P(), P())
    return jax.shard_map(
        shards,
        mesh=mesh,
        in_specs=placed,
        out_specs=(P("dev", None, None), P("dev", None, None)),
        check_vma=False,
    )
```

profile of v0, /device:TPU:0, one launch (start us, length us, event | category | flops | bytes accessed | tf_op | source)
XLA Modules:
  0.0 643.8 jit_solution(5911055930235017972)
XLA Ops:
  7.2 2.8 copy.155
  9.9 7.4 %all-to-all-start = ((bf16[2,128,1280]{2,0,1:T(2,128)(2,1)}), bf16[2,128,1280]{2,0,1:T(2,128)(2,1)}, u32[]{:S(2)}, u32[]{:S(2)}) async-start(bf16[2,128,1280]{2,0,1:T(2,128)(2,1)} %copy.155), calls=%async_computation | async-start | bytes 1310720 | tf_op jit(solution)/shard_map/all_to_all | solution.py:96
  17.7 17.6 %all-to-all-done = bf16[2,128,1280]{2,0,1:T(2,128)(2,1)} async-done(((bf16[2,128,1280]{2,0,1:T(2,128)(2,1)}), bf16[2,128,1280]{2,0,1:T(2,128)(2,1)}, u32[]{:S(2)}, u32[]{:S(2)}) %all-to-all-start) | async-done | bytes 655392 | tf_op jit(solution)/shard_map/all_to_all | solution.py:96
  35.3 2.2 copy.156
  37.4 3.0 gather_fusion.1
  40.5 2.3 broadcast_select_fusion
  42.8 3.6 all-to-all-start.1
  48.1 16.3 %all-to-all-done.1 = bf16[64,4,1280]{2,1,0:T(4,128)(2,1)} async-done(((bf16[64,4,1280]{2,1,0:T(4,128)(2,1)}), bf16[64,4,1280]{2,1,0:T(4,128)(2,1)}, u32[]{:S(2)}, u32[]{:S(2)}) %all-to-all-start.1) | async-done | bytes 655392 | tf_op jit(solution)/shard_map/all_to_all | solution.py:99
  64.3 2.3 fusion.52
  66.7 1.3 copy.160
  68.0 2.2 reshape_reshape.4
  70.2 4.0 convolution_convert_fusion.2
  74.2 3.3 reshape.404
  77.5 2.6 copy.164
  80.1 4.0 convolution_convert_fusion.1
  84.1 2.0 rev.20
  86.1 2.2 copy.163
  88.3 2.0 fusion.56
  90.7 1.4 divide_convert_fusion
  92.1 1.2 copy-done.20
  93.5 1.9 convolution_convert_fusion.3
  95.3 2.0 rev.18
  97.3 2.2 copy.161
  99.5 2.5 copy.159
  102.5 1.1 fusion.23
  105.6 1.9 convolution_convert_fusion
  107.5 2.3 copy.168
  109.7 2.7 reshape.372
  112.4 2.9 convolution_convert_fusion.5
  116.1 1.3 convert_reduce_fusion
  117.4 2.1 convolution_convert_fusion.6
  119.6 2.0 fusion.26
  121.6 3.8 convolution_bitcast_fusion
  127.0 1.8 copy.171
  128.9 2.8 fusion.35
  131.7 11.9 %pad_maximum_fusion = f32[1280,5120]{1,0:T(8,128)} fusion(f32[1280,1280]{1,0:T(8,128)} %convolution_bitcast_fusion, f32[1280,3840]{1,0:T(8,128)S(1)} %fusion.35), kind=kLoop, calls=%fused_computation.2 | loop fusion | flops 6553600 | bytes 52428800 | tf_op jit(solution)/shard_map/concatenate | solution.py:87
  143.5 31.9 %reshape.381 = f32[1280,4,1280]{2,1,0:T(4,128)} reshape(f32[1280,5120]{1,0:T(8,128)} %pad_maximum_fusion) | data formatting | bytes 52428800 | tf_op jit(solution)/shard_map/reshape | solution.py:88
  175.5 6.2 fusion
  181.9 1.0 copy.180
  182.9 50.1 %all_to_all.66 = f32[2,128,1280]{2,0,1:T(2,128)S(1)} all-to-all(f32[2,128,1280]{2,0,1:T(2,128)S(1)} %copy.180), channel_id=1, replica_groups=mesh['dev'=32] {'dev'}, dimensions={1} | all-to-all | bytes 2621440 | tf_op jit(solution)/shard_map/all_to_all | solution.py:111
  233.3 0.9 fusion.19
  234.3 1.9 copy.183
  236.2 3.4 all-to-all-start.3
  239.6 46.3 %all-to-all-done.3 = f32[64,4,1280]{2,1,0:T(4,128)} async-done(((f32[64,4,1280]{2,1,0:T(4,128)}), f32[64,4,1280]{2,1,0:T(4,128)}, u32[]{:S(2)}, u32[]{:S(2)}) %all-to-all-start.3) | async-done | bytes 1310752 | tf_op jit(solution)/shard_map/all_to_all | solution.py:122
  285.9 2.6 copy.184
  288.5 2.7 all_to_all.61
  291.2 343.7 %all-reduce.3.cloned.1.call-done = f32[1280,4,1280]{2,1,0:T(4,128)} async-done(((f32[1280,4,1280]{2,1,0:T(4,128)}), f32[1280,4,1280]{2,1,0:T(4,128)}) %all-reduce.3.cloned.1.call-update) | async-done | bytes 26214416
  634.8 2.1 constant_dynamic-slice_fusion
  (78 shorter events, 6.6 us)
Async XLA Ops:
  7.2 95.3 %copy-start = (bf16[1280,1280]{1,0:T(8,128)(2,1)S(1)}, bf16[1280,1280]{1,0:T(8,128)(2,1)}, u32[]{:S(2)}) copy-start(bf16[1280,1280]{1,0:T(8,128)(2,1)} %param.16) | copy-start | bytes 9830404
  7.2 10.2 %copy-start.19 = (s32[32,2]{0,1:T(2,128)S(1)}, s32[32,2]{0,1:T(2,128)}, u32[]{:S(2)}) copy-start(s32[32,2]{0,1:T(2,128)} %param.11) | copy-start | bytes 772
  9.9 25.3 %all-to-all-start = ((bf16[2,128,1280]{2,0,1:T(2,128)(2,1)}), bf16[2,128,1280]{2,0,1:T(2,128)(2,1)}, u32[]{:S(2)}, u32[]{:S(2)}) async-start(bf16[2,128,1280]{2,0,1:T(2,128)(2,1)} %copy.155), calls=%async_computation | async-start | bytes 1310720 | tf_op jit(solution)/shard_map/all_to_all | solution.py:96
  37.4 9.1 %copy-start.2 = (s32[64]{0:T(128)S(1)}, s32[64]{0:T(128)}, u32[]{:S(2)}) copy-start(s32[64]{0:T(128)} %param.10) | copy-start | bytes 772
  42.8 21.5 %all-to-all-start.1 = ((bf16[64,4,1280]{2,1,0:T(4,128)(2,1)}), bf16[64,4,1280]{2,1,0:T(4,128)(2,1)}, u32[]{:S(2)}, u32[]{:S(2)}) async-start(bf16[64,4,1280]{2,1,0:T(4,128)(2,1)} %broadcast_select_fusion), calls=%async_computation.1 | async-start | bytes 1310720 | tf_op jit(solution)/shard_map/all_to_all | solution.py:99
  46.4 588.4 %all-reduce.3.cloned.1.call-start = ((), (), s32[]{:S(2)}) async-start(), calls=%async_computation.4 | async-start | bytes 52428800
  90.3 1.8 copy-start.3
  90.3 3.1 copy-start.20
  90.7 2.8 copy-start.12
  99.5 2.5 copy-start.7
  99.5 2.5 copy-start.9
  102.5 1.1 copy-start.5
  102.5 1.5 copy-start.18
  107.5 4.9 copy-start.8
  109.7 5.5 copy-start.4
  112.4 2.9 copy-start.10
  112.4 2.9 copy-start.11
  116.1 1.3 copy-start.15
  117.4 2.2 copy-start.16
  119.6 2.0 copy-start.6
  121.6 3.8 copy-start.14
  125.4 1.1 copy-start.17
  126.8 2.1 copy-start.13
  236.2 49.7 %all-to-all-start.3 = ((f32[64,4,1280]{2,1,0:T(4,128)}), f32[64,4,1280]{2,1,0:T(4,128)}, u32[]{:S(2)}, u32[]{:S(2)}) async-start(f32[64,4,1280]{2,1,0:T(4,128)} %copy.183), calls=%async_computation.3 | async-start | bytes 2621440 | tf_op jit(solution)/shard_map/all_to_all | solution.py:122
  285.8 351.1 %copy-start.1 = (bf16[1280,1280]{1,0:T(8,128)(2,1)S(1)}, bf16[1280,1280]{1,0:T(8,128)(2,1)}, u32[]{:S(2)}) copy-start(bf16[1280,1280]{1,0:T(8,128)(2,1)} %param.16) | copy-start | bytes 9830404
Sparse Core Ops, SparseCore 0:
  175.6 459.1 all-reduce.2
where the time goes:
time: 646 us; the launch traced here: 644 us
  waiting for transfers between devices  424 us (66%)
  local copies, waits for them, and re-layouts  81.9 us (13%)
  blocking collectives  50.1 us (8%)
  matrix products  36.9 us (6%)
  other arithmetic  20.9 us (3%)
  between operations  15.8 us (2%)
  starting transfers between devices  14.5 us (2%)
    unnamed x2, waiting for transfers between devices  344 us
    all_to_all x1, blocking collectives, shards(): lax.all_to_all(slot_grads, 'dev', split_axis=1, concat_axis=0, tiled=True)  50.1 us
    all_to_all x1, waiting for transfers between devices, shards(): lax.all_to_all(summed, 'dev', split_axis=0, concat_axis=1, tiled=True)  46.3 us
    reshape x1, local copies, waits for them, and re-layouts, weight_grads(): return joined.reshape(flat_x.shape[1], 4, d_out.shape[1])  31.9 us
    all_to_all x1, waiting for transfers between devices, shards(): lax.all_to_all(embeddings, 'dev', split_axis=1, concat_axis=0, tiled=True)  17.6 us
    all_to_all x1, waiting for transfers between devices, shards(): lax.all_to_all(picked, 'dev', split_axis=0, concat_axis=1, tiled=True)  16.3 us
  transfers between devices with their start and end apart: 4, of which 4 were waited for; matrix products, arithmetic and copies ran while one was open for 2% of the time, Pallas kernels for 0%

commit v1 on v0

v1 whole, which is shorter than its diff:
```python
import functools

import jax
import jax.numpy as jnp
from jax import lax
from jax.experimental import pallas as pl
from jax.experimental.pallas import tpu as pltpu
from jax.sharding import PartitionSpec as P

HEADS = 16
BF = jnp.bfloat16
F32 = jnp.float32
NT = (((1,), (1,)), ((), ()))
TN = (((0,), (0,)), ((), ()))
NN = (((1,), (0,)), ((), ()))


def mm(a, b, dims=NN):
    return lax.dot_general(a, b, dims, preferred_element_type=F32)


def split(value, pieces):
    parts = []
    for _ in range(pieces):
        part = value.astype(BF)
        parts.append(part)
        value = value - part.astype(F32)
    return parts


def local_kernel(
    lens_ref, label_ref, x_ref, wq_ref, wk_ref, wv_ref, wo_ref, wc_ref,
    din_ref, dq_ref, dk_ref, small_ref,
    q_s, k_s, v_s, dv_s, p_s, cs_s, dqa_s, dka_s, dm_s,
):
    rows, width = x_ref.shape
    length = rows // 2
    hd = width // HEADS
    scale = hd ** (-0.5)
    step = 256
    x = x_ref[...]

    def project(n, carry):
        sl = pl.ds(pl.multiple_of(n * step, step), step)
        q_s[:, sl] = mm(x, wq_ref[:, sl]).astype(BF)
        k_s[:, sl] = mm(x, wk_ref[:, sl]).astype(BF)
        v_s[:, sl] = mm(x, wv_ref[:, sl]).astype(BF)
        return carry

    lax.fori_loop(0, width // step, project, 0)

    def window(h):
        first = (h * hd) // 128 * 128
        last = -(-(h * hd + hd) // 128) * 128
        return first, last

    def head_mask(h):
        first, last = window(h)
        lane = lax.broadcasted_iota(jnp.int32, (length, last - first), 1) + first
        return (lane >= h * hd) & (lane < h * hd + hd)

    def side(ref, s, first=0, last=width):
        return ref[s * length:(s + 1) * length, first:last]

    key_lane = lax.broadcasted_iota(jnp.int32, (length, length), 1)
    row_ids = lax.broadcasted_iota(jnp.int32, (length, 1), 0)
    for s in range(2):
        key_ok = key_lane < lens_ref[1 - s]
        live = (row_ids < lens_ref[s]).astype(F32)
        for h in range(HEADS):
            first, last = window(h)
            keys = side(k_s, 1 - s, first, last)
            keys = jnp.where(head_mask(h), keys, jnp.zeros_like(keys))
            scores = mm(side(q_s, s, first, last), keys, NT) * scale
            scores = jnp.where(key_ok, scores, -1000000000.0)
            expo = jnp.exp(scores - jnp.max(scores, axis=1, keepdims=True))
            probs = expo / jnp.sum(expo, axis=1, keepdims=True)
            p_s[s * HEADS + h] = probs
            rounded = probs.astype(BF).astype(F32)
            cs_s[s * HEADS + h:s * HEADS + h + 1, :] = jnp.sum(
                rounded * live, axis=0, keepdims=True
            )

    lane16 = lax.broadcasted_iota(jnp.int32, (HEADS, width), 1)
    head16 = lax.broadcasted_iota(jnp.int32, (HEADS, width), 0)
    own16 = (lane16 >= head16 * hd) & (lane16 < head16 * hd + hd)

    sum_x, ctx_sum, pieces = [], [], []
    for s in range(2):
        col_hi, col_lo = split(cs_s[s * HEADS:(s + 1) * HEADS, :], 2)
        other_v = side(v_s, 1 - s)
        full = mm(col_hi, other_v) + mm(col_lo, other_v)
        ctx = jnp.sum(jnp.where(own16, full, 0.0), axis=0, keepdims=True)
        ctx_sum.append(ctx)
        pieces += [part.astype(F32) for part in split(ctx, 3)]
        slot = lax.broadcasted_iota(jnp.int32, (8, length), 1)
        valid = (slot < lens_ref[s]).astype(F32).astype(BF)
        sum_x.append(mm(valid, side(x_ref, s))[0:1, :])
        other_x = side(x_ref, 1 - s)
        small_ref[s * HEADS:(s + 1) * HEADS, :] = (
            mm(col_hi, other_x) + mm(col_lo, other_x)
        ).astype(BF)
    zero = jnp.zeros((1, width), F32)
    stacked = jnp.concatenate(pieces + [zero, zero], axis=0).astype(BF)
    proj = mm(stacked, wo_ref[...])
    wc = wc_ref[...]
    pooled, lens = [], []
    for s in range(2):
        lens.append(jnp.full((1, 1), lens_ref[s], jnp.int32).astype(F32))
        out = proj[3 * s:3 * s + 1] + proj[3 * s + 1:3 * s + 2] + proj[3 * s + 2:3 * s + 3]
        pooled.append((sum_x[s] + out) / lens[s])
    logit = jnp.sum(wc * pooled[0] * pooled[1], axis=1, keepdims=True)
    label = jnp.full((1, 1), label_ref[0], jnp.int32).astype(F32)
    slope = 1.0 / (1.0 + jnp.exp(-logit)) - label
    d_mixed = [slope * wc * pooled[1 - s] / lens[s] for s in range(2)]
    d_rows = jnp.concatenate(d_mixed + [zero] * 6, axis=0)
    dm_s[...] = d_rows
    d_out = d_rows.astype(BF)
    d_ctx = mm(d_out, wo_ref[...], NT)
    tail = jnp.concatenate(
        ctx_sum + [d_out.astype(F32)[0:2], d_ctx[0:2], zero, zero], axis=0
    )
    small_ref[2 * HEADS:2 * HEADS + 8, :] = tail.astype(BF)

    dqa_s[...] = jnp.zeros_like(dqa_s)
    dka_s[...] = jnp.zeros_like(dka_s)
    for s in range(2):
        o = 1 - s
        grad = jnp.broadcast_to(d_ctx[s:s + 1], (HEADS, width))
        grad = jnp.where(own16, grad, 0.0).astype(BF)
        col_hi, col_lo = split(cs_s[s * HEADS:(s + 1) * HEADS, :], 2)
        dv_s[o * length:(o + 1) * length, :] = (
            mm(col_hi, grad, TN) + mm(col_lo, grad, TN)
        ).astype(BF)
        d_probs = mm(grad, side(v_s, o), NT).astype(BF).astype(F32)
        live = (row_ids < lens_ref[s]).astype(F32) * scale
        for h in range(HEADS):
            first, last = window(h)
            mask = head_mask(h)
            probs = p_s[s * HEADS + h]
            term = probs * d_probs[h:h + 1, :]
            total = jnp.sum(term, axis=1, keepdims=True)
            d_scores = ((term - probs * total) * live).astype(BF)
            keys = side(k_s, o, first, last)
            query = side(q_s, s, first, last)
            keys = jnp.where(mask, keys, jnp.zeros_like(keys))
            query = jnp.where(mask, query, jnp.zeros_like(query))
            dqa_s[s * length:(s + 1) * length, first:last] += mm(d_scores, keys)
            dka_s[o * length:(o + 1) * length, first:last] += mm(d_scores, query, TN)
    dq_ref[...] = dqa_s[...].astype(BF)
    dk_ref[...] = dka_s[...].astype(BF)

    def back(n, carry):
        sl = pl.ds(pl.multiple_of(n * step, step), step)
        total = mm(dq_ref[...], wq_ref[sl, :], NT)
        total = total + mm(dk_ref[...], wk_ref[sl, :], NT)
        total = total + mm(dv_s[...], wv_ref[sl, :], NT)
        for s in range(2):
            live = row_ids < lens_ref[s]
            mixed = jnp.where(live, dm_s[s:s + 1, sl], 0.0)
            din_ref[s * length:(s + 1) * length, sl] = (
                total[s * length:(s + 1) * length] + mixed
            ).astype(BF)
        return carry

    lax.fori_loop(0, width // step, back, 0)


def local_step(x, lens, label, wq, wk, wv, wo, wc):
    rows, width = x.shape
    length = rows // 2
    vmem = pl.BlockSpec(memory_space=pltpu.VMEM)
    smem = pl.BlockSpec(memory_space=pltpu.SMEM)
    like = jax.ShapeDtypeStruct((rows, width), BF)
    return pl.pallas_call(
        local_kernel,
        out_shape=(like, like, like, jax.ShapeDtypeStruct((2 * HEADS + 8, width), BF)),
        in_specs=[smem, smem] + [vmem] * 6,
        out_specs=(vmem,) * 4,
        scratch_shapes=[
            pltpu.VMEM((rows, width), BF),
            pltpu.VMEM((rows, width), BF),
            pltpu.VMEM((rows, width), BF),
            pltpu.VMEM((rows, width), BF),
            pltpu.VMEM((2 * HEADS, length, length), F32),
            pltpu.VMEM((2 * HEADS, length), F32),
            pltpu.VMEM((rows, width), F32),
            pltpu.VMEM((rows, width), F32),
            pltpu.VMEM((8, width), F32),
        ],
        compiler_params=pltpu.CompilerParams(vmem_limit_bytes=48 * 1024 * 1024),
        cost_estimate=pl.CostEstimate(
            flops=6 * 2 * rows * width * width,
            bytes_accessed=4 * 2 * width * width + 8 * 2 * rows * width,
            transcendentals=2 * HEADS * length * length,
        ),
    )(lens, label, x, wq, wk, wv, wo, wc.reshape(1, width))


def swap(value, n, bit):
    return lax.ppermute(value, "dev", [(i, i ^ (1 << bit)) for i in range(n)])


def halve(part, me, n, order):
    bits = (n // 2).bit_length() - 1
    cols = part.shape[-2:]
    part = part.reshape((2,) * bits + part.shape[1:])
    left = list(range(bits, 0, -1))
    for turn, bit in enumerate(order):
        axis = left.index(bit)
        mine = (me >> bit) & 1
        keep = lax.dynamic_index_in_dim(part, mine, axis, keepdims=False)
        send = lax.dynamic_index_in_dim(part, 1 - mine, axis, keepdims=False)
        got = swap(send, n, bit)
        part = keep.astype(F32) + got.astype(F32)
        if turn < len(order) - 1:
            part = part.astype(BF)
        left.pop(axis)
    return part.reshape((2,) + cols)


def shards(n, embeddings, lengths, pairs, labels, w_query, w_key, w_value, w_out, w_class):
    length = embeddings.shape[1]
    width = embeddings.shape[2]
    chain_total = lengths.shape[0]
    me = lax.axis_index("dev")
    spread = lax.all_to_all(embeddings, "dev", split_axis=1, concat_axis=0, tiled=True)
    slot_ids = pairs.reshape(-1)
    picked = spread.at[slot_ids].get(mode="promise_in_bounds")
    gathered = lax.all_to_all(picked, "dev", split_axis=0, concat_axis=1, tiled=True)
    x = gathered.reshape(2 * length, width)
    my_pair = lax.dynamic_index_in_dim(pairs, me, 0, keepdims=False)
    chain_lens = lengths.at[my_pair].get(mode="promise_in_bounds")

    x_other = swap(x, n, 0)
    d_input, d_query, d_keys, small = local_step(
        x, chain_lens, labels, w_query, w_key, w_value, w_out, w_class
    )

    core = me & 1
    first = core == 0
    own = jnp.where(first, d_query, d_keys)
    theirs = swap(jnp.where(first, d_keys, d_query), n, 0)
    factors = lax.all_gather(small, "dev", axis=0, tiled=False)

    chips = n // 2
    block = width // n
    bits = chips.bit_length() - 1
    orders = [list(range(1, bits + 1))]
    if bits >= 4:
        orders = [
            [1, 2] + list(range(3, bits + 1)),
            [2, 1] + list(range(3, bits + 1)),
            list(range(3, bits + 1)) + [1, 2],
        ]
    cuts = [0, width] if len(orders) == 1 else [0, 512, 1024, width]
    sums = []
    for order, lo, hi in zip(orders, cuts[:-1], cuts[1:]):
        part = mm(x, own[:, lo:hi], TN) + mm(x_other, theirs[:, lo:hi], TN)
        part = part.astype(BF).reshape(chips, 2, block, hi - lo)
        sums.append(halve(part, me, n, order))
    chip_sum = jnp.concatenate(sums, axis=-1)
    kept = lax.dynamic_index_in_dim(chip_sum, core, 0, keepdims=False)
    passed = lax.dynamic_index_in_dim(chip_sum, 1 - core, 0, keepdims=False)
    got = swap(passed.astype(BF), n, 0).astype(F32)
    d_wq = jnp.where(first, kept, got)
    d_wk = jnp.where(first, got, kept)

    slot_grads = d_input.reshape(2, length, width)
    by_rows = lax.all_to_all(slot_grads, "dev", split_axis=1, concat_axis=0, tiled=True)
    row_block = by_rows.shape[1]
    chain_index = jnp.arange(chain_total, dtype=jnp.int32)
    selector = (chain_index[:, None] == slot_ids[None, :]).astype(BF)
    summed = mm(selector, by_rows.reshape(slot_ids.shape[0], row_block * width)).astype(BF)
    summed = summed.reshape(chain_total, row_block, width)
    d_embeddings = lax.all_to_all(summed, "dev", split_axis=0, concat_axis=1, tiled=True)

    mine = lax.dynamic_slice_in_dim(factors, me * block, block, 2)
    tail = 2 * HEADS
    head_of = jnp.arange(width, dtype=jnp.int32) // (width // HEADS)
    own_head = head_of[None, :] == jnp.arange(HEADS, dtype=jnp.int32)[:, None]
    grads = factors[:, tail + 4:tail + 6]
    spread_grads = jnp.where(own_head, grads[:, :, None, :], jnp.zeros((), BF))
    d_wv = mm(
        mine[:, :tail].reshape(n * tail, block), spread_grads.reshape(n * tail, width), TN
    )
    d_wo = mm(
        mine[:, tail:tail + 2].reshape(n * 2, block),
        factors[:, tail + 2:tail + 4].reshape(n * 2, width),
        TN,
    )
    d_weights = jnp.stack([d_wq, d_wk, d_wv, d_wo], axis=1)
    return (d_embeddings.astype(F32), d_weights)


def solution(mesh):
    placed = (P("dev", None, None), P(), P(), P("dev"), P(), P(), P(), P(), P())
    return jax.shard_map(
        functools.partial(shards, mesh.shape["dev"]),
        mesh=mesh,
        in_specs=placed,
        out_specs=(P("dev", None, None), P("dev", None, None)),
        check_vma=False,
    )
```

time: 646 us -> 194 us (0.30)
  waiting for transfers between devices: 424 us -> 94.5 us
  local copies, waits for them, and re-layouts: 81.9 us -> 20.9 us
  blocking collectives: 50.1 us -> 0 us
  matrix products: 36.9 us -> 8.72 us
  starting transfers between devices: 14.5 us -> 33 us
  Pallas kernels: 0 us -> 16.7 us
  other arithmetic: 20.9 us -> 4.54 us
    unnamed x2 -> x1, waiting for transfers between devices: 344 us -> 0.02 us
    ppermute x0 -> x15, waiting for transfers between devices: none -> 60.6 us  [swap(): return lax.ppermute(value, 'dev', [(i, i ^ 1 << bit) for i in range(n)])]
    all_to_all x1 -> x0, blocking collectives: 50.1 us -> none  [shards(): lax.all_to_all(slot_grads, 'dev', split_axis=1, concat_axis=0, tiled=True)]
    all_to_all x1, waiting for transfers between devices: 46.3 us -> 0.01 us  [shards(): lax.all_to_all(summed, 'dev', split_axis=0, concat_axis=1, tiled=True)]
    reshape x6 -> x4, local copies, waits for them, and re-layouts: 35.5 us -> 2.98 us  [the longest x1 1.51 us: shards(): slot_grads = d_input.reshape(2, length, width)]
    dot_general x15 -> x9, matrix products: 36.9 us -> 8.72 us  [mm(): return lax.dot_general(a, b, dims, preferred_element_type=F32)]
    pallas_call x0 -> x1, Pallas kernels: none -> 16.7 us  [local_step(): pl.pallas_call(local_kernel, out_shape=(like, like, like, jax.ShapeDtypeS...]
    ppermute x0 -> x15, starting transfers between devices: none -> 14.4 us  [swap(): return lax.ppermute(value, 'dev', [(i, i ^ 1 << bit) for i in range(n)])]
  transfers between devices with their start and end apart: 4 -> 20, of which waited for: 4 -> 13; matrix products, arithmetic and copies ran while one was open for 2% -> 11% of each run, Pallas kernels for 0% -> 9%
where the time goes in v1:
time: 194 us
  waiting for transfers between devices  94.5 us (49%)
  starting transfers between devices  33 us (17%)
  local copies, waits for them, and re-layouts  20.9 us (11%)
  Pallas kernels  16.7 us (9%)
  between operations  15.2 us (8%)
  matrix products  8.72 us (4%)
  other arithmetic  4.54 us (2%)
    ppermute x15, waiting for transfers between devices, swap(): return lax.ppermute(value, 'dev', [(i, i ^ 1 << bit) for i in range(n)])  60.6 us
    all_to_all x1, waiting for transfers between devices, shards(): lax.all_to_all(embeddings, 'dev', split_axis=1, concat_axis=0, tiled=True)  17.7 us
    pallas_call x1, Pallas kernels, local_step(): pl.pallas_call(local_kernel, out_shape=(like, like, like, jax.ShapeDtypeS...  16.7 us
    all_to_all x1, waiting for transfers between devices, shards(): lax.all_to_all(picked, 'dev', split_axis=0, concat_axis=1, tiled=True)  16.2 us
    ppermute x15, starting transfers between devices, swap(): return lax.ppermute(value, 'dev', [(i, i ^ 1 << bit) for i in range(n)])  14.4 us
    dot_general x9, matrix products, mm(): return lax.dot_general(a, b, dims, preferred_element_type=F32)  8.72 us
    all_to_all x1, starting transfers between devices, shards(): lax.all_to_all(embeddings, 'dev', split_axis=1, concat_axis=0, tiled=True)  7.3 us
    unnamed x14, local copies, waits for them, and re-layouts  6.34 us
  transfers between devices with their start and end apart: 20, of which 13 were waited for; matrix products, arithmetic and copies ran while one was open for 11% of the time, Pallas kernels for 9%

profile of v1, /device:TPU:0, one launch (start us, length us, event | category | flops | bytes accessed | tf_op | source)
XLA Modules:
  0.0 193.5 jit_solution(11223779046139258060)
XLA Ops:
  7.2 2.6 %copy.56 = bf16[2,128,1280]{2,0,1:T(2,128)(2,1)} copy(bf16[2,128,1280]{2,1,0:T(8,128)(2,1)} %param.9) | data formatting | bytes 1310720 | tf_op args[0]
  9.8 7.3 %all-to-all-start = ((bf16[2,128,1280]{2,0,1:T(2,128)(2,1)}), bf16[2,128,1280]{2,0,1:T(2,128)(2,1)S(1)}, u32[]{:S(2)}, u32[]{:S(2)}) async-start(bf16[2,128,1280]{2,0,1:T(2,128)(2,1)} %copy.56), calls=%async_computation | async-start | bytes 1310720 | tf_op jit(solution)/shard_map/all_to_all | solution.py:227
  17.3 17.7 %all-to-all-done = bf16[2,128,1280]{2,0,1:T(2,128)(2,1)S(1)} async-done(((bf16[2,128,1280]{2,0,1:T(2,128)(2,1)}), bf16[2,128,1280]{2,0,1:T(2,128)(2,1)S(1)}, u32[]{:S(2)}, u32[]{:S(2)}) %all-to-all-start) | async-done | bytes 655392 | tf_op jit(solution)/shard_map/all_to_all | solution.py:227
  35.3 1.9 gather_fusion.1
  37.2 3.5 %all-to-all-start.1 = ((bf16[64,4,1280]{2,1,0:T(4,128)(2,1)}), bf16[64,4,1280]{2,1,0:T(4,128)(2,1)S(1)}, u32[]{:S(2)}, u32[]{:S(2)}) async-start(bf16[64,4,1280]{2,1,0:T(4,128)(2,1)} %gather_fusion.1), calls=%async_computation.1 | async-start | bytes 1310720 | tf_op jit(solution)/shard_map/all_to_all | solution.py:230
  41.8 0.6 gather_fusion
  42.4 16.2 %all-to-all-done.1 = bf16[64,4,1280]{2,1,0:T(4,128)(2,1)S(1)} async-done(((bf16[64,4,1280]{2,1,0:T(4,128)(2,1)}), bf16[64,4,1280]{2,1,0:T(4,128)(2,1)S(1)}, u32[]{:S(2)}, u32[]{:S(2)}) %all-to-all-start.1) | async-done | bytes 655392 | tf_op jit(solution)/shard_map/all_to_all | solution.py:230
  59.2 1.9 copy-done.1
  61.1 16.7 %shard_map.104 = (bf16[256,1280]{1,0:T(8,128)(2,1)S(1)}, bf16[256,1280]{1,0:T(8,128)(2,1)S(1)}, bf16[256,1280]{1,0:T(8,128)(2,1)S(1)}, bf16[40,1280]{1,0:T(8,128)(2,1)}) custom-call(s32[2]{0:T(128)S(1)} %gather_fusion, s32[1]{0:T(128)S(6)} %copy.103.label_ref, bf16[256,1280]{1,0:T(8,128)(2,1)S(1)} %reshape.143.x_ref, bf16[1280,1280]{1,0:T(8,128)(2,1)S(1)} %copy-done.1, ...), custom_call_target="tpu_custom_call" | custom-call | flops 5033164800 | bytes 18350080 | tf_op jit(solution)/shard_map/pallas_call | solution.py:175
  77.8 0.9 broadcast_select_fusion.1
  80.0 1.5 copy.60
  81.5 3.8 %all-to-all-start.2 = ((bf16[2,128,1280]{2,0,1:T(2,128)(2,1)}), bf16[2,128,1280]{2,0,1:T(2,128)(2,1)}, u32[]{:S(2)}, u32[]{:S(2)}) async-start(bf16[2,128,1280]{2,0,1:T(2,128)(2,1)} %copy.60), calls=%async_computation.2 | async-start | bytes 1310720 | tf_op jit(solution)/shard_map/all_to_all | solution.py:270
  85.4 1.5 fusion.15
  86.8 1.5 fusion.12
  88.4 1.3 fusion.2
  89.7 1.6 collective-permute-start.10
  91.3 1.5 fusion
  93.0 1.5 collective-permute-start.2
  94.5 13.1 %collective-permute-done.10 = bf16[2,2,2,2,40,256]{5,4,3,1,2,0:T(8,128)(2,1)S(1)} collective-permute-done((bf16[2,2,2,2,40,256]{5,4,3,1,2,0:T(8,128)(2,1)S(1)}, bf16[2,2,2,2,40,256]{5,4,3,1,2,0:T(8,128)(2,1)S(1)}, u32[]{:S(2)}, u32[]{:S(2)}) %collective-permute-start.10) | collective-permute-done | bytes 327712 | tf_op jit(solution)/shard_map/ppermute | solution.py:201
  107.8 2.5 %collective-permute-start.11 = (bf16[2,2,2,40,256]{4,3,2,0,1:T(8,128)(2,1)S(1)}, bf16[2,2,2,40,256]{4,3,2,0,1:T(8,128)(2,1)S(1)}, u32[]{:S(2)}, u32[]{:S(2)}) collective-permute-start(bf16[2,2,2,40,256]{4,3,2,0,1:T(8,128)(2,1)S(1)} %dynamic-slice_bitcast_fusion.2), channel_id=1, source_target_pairs={{0,16},{1,17},{2,18},{3,19},{4,20},{5,21},{6,22},{7,23},{8,24},{9,... | collective-permute-start | bytes 491528 | tf_op jit(solution)/shard_map/ppermute | solution.py:201
  110.2 1.5 fusion.1
  111.7 9.1 %collective-permute-done.11 = bf16[2,2,2,40,256]{4,3,2,0,1:T(8,128)(2,1)S(1)} collective-permute-done((bf16[2,2,2,40,256]{4,3,2,0,1:T(8,128)(2,1)S(1)}, bf16[2,2,2,40,256]{4,3,2,0,1:T(8,128)(2,1)S(1)}, u32[]{:S(2)}, u32[]{:S(2)}) %collective-permute-start.11) | collective-permute-done | bytes 163872 | tf_op jit(solution)/shard_map/ppermute | solution.py:201
  120.9 1.6 collective-permute-start.12
  122.6 0.9 copy.100
  123.5 1.5 collective-permute-start.6
  125.4 1.6 collective-permute-start.13
  127.0 1.3 copy.61
  128.8 1.3 reshape.147
  130.1 3.9 %all-to-all-start.3 = ((bf16[64,4,1280]{2,1,0:T(4,128)(2,1)}), bf16[64,4,1280]{2,1,0:T(4,128)(2,1)S(1)}, u32[]{:S(2)}, u32[]{:S(2)}) async-start(bf16[64,4,1280]{2,1,0:T(4,128)(2,1)} %reshape.147), calls=%async_computation.3 | async-start | bytes 1310720 | tf_op jit(solution)/shard_map/all_to_all | solution.py:276
  134.0 18.1 %collective-permute-done.13 = bf16[2,40,256]{2,1,0:T(8,128)(2,1)S(1)} collective-permute-done((bf16[2,40,256]{2,1,0:T(8,128)(2,1)S(1)}, bf16[2,40,256]{2,1,0:T(8,128)(2,1)S(1)}, u32[]{:S(2)}, u32[]{:S(2)}) %collective-permute-start.13) | collective-permute-done | bytes 40992 | tf_op jit(solution)/shard_map/ppermute | solution.py:201
  152.2 1.3 fusion.4
  153.5 1.8 collective-permute-start.3
  155.4 1.3 fusion.3
  156.7 0.6 collective-permute-start.7
  157.3 4.8 %collective-permute-done.3 = bf16[2,2,2,40,512]{4,3,2,0,1:T(8,128)(2,1)S(1)} collective-permute-done((bf16[2,2,2,40,512]{4,3,2,0,1:T(8,128)(2,1)S(1)}, bf16[2,2,2,40,512]{4,3,2,0,1:T(8,128)(2,1)S(1)}, u32[]{:S(2)}, u32[]{:S(2)}) %collective-permute-start.3) | collective-permute-done | bytes 327712 | tf_op jit(solution)/shard_map/ppermute | solution.py:201
  162.4 2.1 %collective-permute-done.7 = bf16[2,2,2,40,512]{4,3,2,0,1:T(8,128)(2,1)S(1)} collective-permute-done((bf16[2,2,2,40,512]{4,3,2,0,1:T(8,128)(2,1)S(1)}, bf16[2,2,2,40,512]{4,3,2,0,1:T(8,128)(2,1)S(1)}, u32[]{:S(2)}, u32[]{:S(2)}) %collective-permute-start.7) | collective-permute-done | bytes 327712 | tf_op jit(solution)/shard_map/ppermute | solution.py:201
  164.7 3.6 %collective-permute-done.4 = bf16[2,2,40,512]{3,2,1,0:T(8,128)(2,1)S(1)} collective-permute-done((bf16[2,2,40,512]{3,2,1,0:T(8,128)(2,1)S(1)}, bf16[2,2,40,512]{3,2,1,0:T(8,128)(2,1)S(1)}, u32[]{:S(2)}, u32[]{:S(2)}) %collective-permute-start.4) | collective-permute-done | bytes 163872 | tf_op jit(solution)/shard_map/ppermute | solution.py:201
  168.7 2.2 %collective-permute-done.8 = bf16[2,2,40,512]{3,2,1,0:T(8,128)(2,1)S(1)} collective-permute-done((bf16[2,2,40,512]{3,2,1,0:T(8,128)(2,1)S(1)}, bf16[2,2,40,512]{3,2,1,0:T(8,128)(2,1)S(1)}, u32[]{:S(2)}, u32[]{:S(2)}) %collective-permute-start.8) | collective-permute-done | bytes 163872 | tf_op jit(solution)/shard_map/ppermute | solution.py:201
  171.0 0.5 collective-permute-start.9
  171.5 3.2 %collective-permute-done.5 = bf16[2,40,512]{2,1,0:T(8,128)(2,1)S(1)} collective-permute-done((bf16[2,40,512]{2,1,0:T(8,128)(2,1)S(1)}, bf16[2,40,512]{2,1,0:T(8,128)(2,1)S(1)}, u32[]{:S(2)}, u32[]{:S(2)}) %collective-permute-start.5) | collective-permute-done | bytes 81952 | tf_op jit(solution)/shard_map/ppermute | solution.py:201
  174.7 2.6 %collective-permute-done.9 = bf16[2,40,512]{2,1,0:T(8,128)(2,1)S(1)} collective-permute-done((bf16[2,40,512]{2,1,0:T(8,128)(2,1)S(1)}, bf16[2,40,512]{2,1,0:T(8,128)(2,1)S(1)}, u32[]{:S(2)}, u32[]{:S(2)}) %collective-permute-start.9) | collective-permute-done | bytes 81952 | tf_op jit(solution)/shard_map/ppermute | solution.py:201
  177.5 1.3 collective-permute-done.14
  178.9 1.5 reshape.149
  180.4 1.7 fusion.33
  182.1 1.2 constant_dynamic-slice_fusion
  183.3 1.0 constant_dynamic-slice_fusion.1
  184.6 0.6 convolution_bitcast_fusion.1
  185.5 1.2 copy.72
  (73 shorter events, 5.7 us)
Async XLA Ops:
  7.2 34.6 %copy-start = (s32[64]{0:T(128)S(1)}, s32[64]{0:T(128)}, u32[]{:S(2)}) copy-start(s32[64]{0:T(128)} %param.10) | copy-start | bytes 772
  7.2 9.9 %copy-start.4 = (s32[32,2]{0,1:T(2,128)S(1)}, s32[32,2]{0,1:T(2,128)}, u32[]{:S(2)}) copy-start(s32[32,2]{0,1:T(2,128)} %param.11) | copy-start | bytes 772
  9.8 31.3 %copy-start.3 = (f32[1280]{0:T(1024)S(1)}, f32[1280]{0:T(1024)}, u32[]{:S(2)}) copy-start(f32[1280]{0:T(1024)} %param.17) | copy-start | bytes 15364
  9.8 25.2 %all-to-all-start = ((bf16[2,128,1280]{2,0,1:T(2,128)(2,1)}), bf16[2,128,1280]{2,0,1:T(2,128)(2,1)S(1)}, u32[]{:S(2)}, u32[]{:S(2)}) async-start(bf16[2,128,1280]{2,0,1:T(2,128)(2,1)} %copy.56), calls=%async_computation | async-start | bytes 1310720 | tf_op jit(solution)/shard_map/all_to_all | solution.py:227
  37.2 21.4 %all-to-all-start.1 = ((bf16[64,4,1280]{2,1,0:T(4,128)(2,1)}), bf16[64,4,1280]{2,1,0:T(4,128)(2,1)S(1)}, u32[]{:S(2)}, u32[]{:S(2)}) async-start(bf16[64,4,1280]{2,1,0:T(4,128)(2,1)} %gather_fusion.1), calls=%async_computation.1 | async-start | bytes 1310720 | tf_op jit(solution)/shard_map/all_to_all | solution.py:230
  40.7 139.7 %all-gather.3.cloned.1.call-start = ((), (), s32[]{:S(2)}) async-start(), calls=%async_computation.4 | async-start | bytes 3379200 | tf_op jit(solution)/shard_map/all_gather | solution.py:244
  59.0 29.3 %collective-permute-start = (bf16[256,1280]{1,0:T(8,128)(2,1)S(1)}, bf16[256,1280]{1,0:T(8,128)(2,1)S(1)}, u32[]{:S(2)}, u32[]{:S(2)}) collective-permute-start(bf16[256,1280]{1,0:T(8,128)(2,1)S(1)} %reshape.143.x_ref), channel_id=1, source_target_pairs={{0,1},{1,0},{2,3},{3,2},{4,5},{5,4},{6,7},{7,6},{8,9},{9,8},{10,11... | collective-permute-start | bytes 1966088 | tf_op jit(solution)/shard_map/ppermute | solution.py:201
  59.2 1.9 copy-start.1
  78.7 0.9 copy-start.2
  78.7 9.6 %collective-permute-start.1 = (bf16[256,1280]{1,0:T(8,128)(2,1)}, bf16[256,1280]{1,0:T(8,128)(2,1)}, u32[]{:S(2)}, u32[]{:S(2)}) collective-permute-start(bf16[256,1280]{1,0:T(8,128)(2,1)} %get-tuple-element.24), channel_id=1, source_target_pairs={{0,1},{1,0},{2,3},{3,2},{4,5},{5,4},{6,7},{7,6},{8,9},{9,8},{10,11... | collective-permute-start | bytes 1966088 | tf_op jit(solution)/shard_map/ppermute | solution.py:201
  81.5 45.5 %all-to-all-start.2 = ((bf16[2,128,1280]{2,0,1:T(2,128)(2,1)}), bf16[2,128,1280]{2,0,1:T(2,128)(2,1)}, u32[]{:S(2)}, u32[]{:S(2)}) async-start(bf16[2,128,1280]{2,0,1:T(2,128)(2,1)} %copy.60), calls=%async_computation.2 | async-start | bytes 1310720 | tf_op jit(solution)/shard_map/all_to_all | solution.py:270
  89.7 17.9 %collective-permute-start.10 = (bf16[2,2,2,2,40,256]{5,4,3,1,2,0:T(8,128)(2,1)S(1)}, bf16[2,2,2,2,40,256]{5,4,3,1,2,0:T(8,128)(2,1)S(1)}, u32[]{:S(2)}, u32[]{:S(2)}) collective-permute-start(bf16[2,2,2,2,40,256]{5,4,3,1,2,0:T(8,128)(2,1)S(1)} %bitcast.135), channel_id=1, source_target_pairs={{0,8},{1,9},{2,10},{3,11},{4,12},{5,13},{6,14},{7,15},{8,0},{9,1},... | collective-permute-start | bytes 983048 | tf_op jit(solution)/shard_map/ppermute | solution.py:201
  93.0 59.2 %collective-permute-start.2 = (bf16[2,2,2,2,40,512]{5,4,3,0,1,2:T(8,128)(2,1)S(1)}, bf16[2,2,2,2,40,512]{5,4,3,0,1,2:T(8,128)(2,1)}, u32[]{:S(2)}, u32[]{:S(2)}) collective-permute-start(bf16[2,2,2,2,40,512]{5,4,3,0,1,2:T(8,128)(2,1)S(1)} %bitcast.134), channel_id=1, source_target_pairs={{0,2},{1,3},{2,0},{3,1},{4,6},{5,7},{6,4},{7,5},{8,10},{9,11},{10,... | collective-permute-start | bytes 1966088 | tf_op jit(solution)/shard_map/ppermute | solution.py:201
  107.8 13.0 %collective-permute-start.11 = (bf16[2,2,2,40,256]{4,3,2,0,1:T(8,128)(2,1)S(1)}, bf16[2,2,2,40,256]{4,3,2,0,1:T(8,128)(2,1)S(1)}, u32[]{:S(2)}, u32[]{:S(2)}) collective-permute-start(bf16[2,2,2,40,256]{4,3,2,0,1:T(8,128)(2,1)S(1)} %dynamic-slice_bitcast_fusion.2), channel_id=1, source_target_pairs={{0,16},{1,17},{2,18},{3,19},{4,20},{5,21},{6,22},{7,23},{8,24},{9,... | collective-permute-start | bytes 491528 | tf_op jit(solution)/shard_map/ppermute | solution.py:201
  120.9 4.5 %collective-permute-start.12 = (bf16[2,2,40,256]{3,2,1,0:T(8,128)(2,1)S(1)}, bf16[2,2,40,256]{3,2,1,0:T(8,128)(2,1)S(1)}, u32[]{:S(2)}, u32[]{:S(2)}) collective-permute-start(bf16[2,2,40,256]{3,2,1,0:T(8,128)(2,1)S(1)} %dynamic-slice_bitcast_fusion.5), channel_id=1, source_target_pairs={{0,2},{1,3},{2,0},{3,1},{4,6},{5,7},{6,4},{7,5},{8,10},{9,11},{10,... | collective-permute-start | bytes 245768 | tf_op jit(solution)/shard_map/ppermute | solution.py:201
  123.5 31.9 %collective-permute-start.6 = (bf16[2,2,2,2,40,512]{5,4,3,0,1,2:T(8,128)(2,1)}, bf16[2,2,2,2,40,512]{5,4,3,0,1,2:T(8,128)(2,1)}, u32[]{:S(2)}, u32[]{:S(2)}) collective-permute-start(bf16[2,2,2,2,40,512]{5,4,3,0,1,2:T(8,128)(2,1)} %bitcast.119), channel_id=1, source_target_pairs={{0,4},{1,5},{2,6},{3,7},{4,0},{5,1},{6,2},{7,3},{8,12},{9,13},{10,... | collective-permute-start | bytes 1966088 | tf_op jit(solution)/shard_map/ppermute | solution.py:201
  125.4 26.7 %collective-permute-start.13 = (bf16[2,40,256]{2,1,0:T(8,128)(2,1)S(1)}, bf16[2,40,256]{2,1,0:T(8,128)(2,1)S(1)}, u32[]{:S(2)}, u32[]{:S(2)}) collective-permute-start(bf16[2,40,256]{2,1,0:T(8,128)(2,1)S(1)} %dynamic-slice_bitcast_fusion.8), channel_id=1, source_target_pairs={{0,4},{1,5},{2,6},{3,7},{4,0},{5,1},{6,2},{7,3},{8,12},{9,13},{10,... | collective-permute-start | bytes 122888 | tf_op jit(solution)/shard_map/ppermute | solution.py:201
  130.1 48.7 %all-to-all-start.3 = ((bf16[64,4,1280]{2,1,0:T(4,128)(2,1)}), bf16[64,4,1280]{2,1,0:T(4,128)(2,1)S(1)}, u32[]{:S(2)}, u32[]{:S(2)}) async-start(bf16[64,4,1280]{2,1,0:T(4,128)(2,1)} %reshape.147), calls=%async_computation.3 | async-start | bytes 1310720 | tf_op jit(solution)/shard_map/all_to_all | solution.py:276
  153.5 8.7 %collective-permute-start.3 = (bf16[2,2,2,40,512]{4,3,2,0,1:T(8,128)(2,1)S(1)}, bf16[2,2,2,40,512]{4,3,2,0,1:T(8,128)(2,1)S(1)}, u32[]{:S(2)}, u32[]{:S(2)}) collective-permute-start(bf16[2,2,2,40,512]{4,3,2,0,1:T(8,128)(2,1)S(1)} %dynamic-slice_bitcast_fusion.1), channel_id=1, source_target_pairs={{0,4},{1,5},{2,6},{3,7},{4,0},{5,1},{6,2},{7,3},{8,12},{9,13},{10,... | collective-permute-start | bytes 983048 | tf_op jit(solution)/shard_map/ppermute | solution.py:201
  156.7 7.7 %collective-permute-start.7 = (bf16[2,2,2,40,512]{4,3,2,0,1:T(8,128)(2,1)S(1)}, bf16[2,2,2,40,512]{4,3,2,0,1:T(8,128)(2,1)S(1)}, u32[]{:S(2)}, u32[]{:S(2)}) collective-permute-start(bf16[2,2,2,40,512]{4,3,2,0,1:T(8,128)(2,1)S(1)} %dynamic-slice_bitcast_fusion), channel_id=1, source_target_pairs={{0,2},{1,3},{2,0},{3,1},{4,6},{5,7},{6,4},{7,5},{8,10},{9,11},{10,... | collective-permute-start | bytes 983048 | tf_op jit(solution)/shard_map/ppermute | solution.py:201
  162.3 6.0 %collective-permute-start.4 = (bf16[2,2,40,512]{3,2,1,0:T(8,128)(2,1)S(1)}, bf16[2,2,40,512]{3,2,1,0:T(8,128)(2,1)S(1)}, u32[]{:S(2)}, u32[]{:S(2)}) collective-permute-start(bf16[2,2,40,512]{3,2,1,0:T(8,128)(2,1)S(1)} %dynamic-slice_bitcast_fusion.4), channel_id=1, source_target_pairs={{0,8},{1,9},{2,10},{3,11},{4,12},{5,13},{6,14},{7,15},{8,0},{9,1},... | collective-permute-start | bytes 491528 | tf_op jit(solution)/shard_map/ppermute | solution.py:201
  164.6 6.4 %collective-permute-start.8 = (bf16[2,2,40,512]{3,2,1,0:T(8,128)(2,1)S(1)}, bf16[2,2,40,512]{3,2,1,0:T(8,128)(2,1)S(1)}, u32[]{:S(2)}, u32[]{:S(2)}) collective-permute-start(bf16[2,2,40,512]{3,2,1,0:T(8,128)(2,1)S(1)} %dynamic-slice_bitcast_fusion.3), channel_id=1, source_target_pairs={{0,8},{1,9},{2,10},{3,11},{4,12},{5,13},{6,14},{7,15},{8,0},{9,1},... | collective-permute-start | bytes 491528 | tf_op jit(solution)/shard_map/ppermute | solution.py:201
  168.4 6.3 %collective-permute-start.5 = (bf16[2,40,512]{2,1,0:T(8,128)(2,1)S(1)}, bf16[2,40,512]{2,1,0:T(8,128)(2,1)S(1)}, u32[]{:S(2)}, u32[]{:S(2)}) collective-permute-start(bf16[2,40,512]{2,1,0:T(8,128)(2,1)S(1)} %dynamic-slice_bitcast_fusion.7), channel_id=1, source_target_pairs={{0,16},{1,17},{2,18},{3,19},{4,20},{5,21},{6,22},{7,23},{8,24},{9,... | collective-permute-start | bytes 245768 | tf_op jit(solution)/shard_map/ppermute | solution.py:201
  171.0 6.3 %collective-permute-start.9 = (bf16[2,40,512]{2,1,0:T(8,128)(2,1)S(1)}, bf16[2,40,512]{2,1,0:T(8,128)(2,1)S(1)}, u32[]{:S(2)}, u32[]{:S(2)}) collective-permute-start(bf16[2,40,512]{2,1,0:T(8,128)(2,1)S(1)} %dynamic-slice_bitcast_fusion.6), channel_id=1, source_target_pairs={{0,16},{1,17},{2,18},{3,19},{4,20},{5,21},{6,22},{7,23},{8,24},{9,... | collective-permute-start | bytes 245768 | tf_op jit(solution)/shard_map/ppermute | solution.py:201
  177.4 1.4 collective-permute-start.14
Sparse Core Ops, SparseCore 0:
  80.1 75.5 all-gather.2

commit v2 on v1

--- a/solution.py
+++ b/solution.py
@@ -29,9 +29,9 @@
 
 
 def local_kernel(
-    lens_ref, label_ref, x_ref, wq_ref, wk_ref, wv_ref, wo_ref, wc_ref,
-    din_ref, dq_ref, dk_ref, small_ref,
-    q_s, k_s, v_s, dv_s, p_s, cs_s, dqa_s, dka_s, dm_s,
+    lens_ref, label_ref, core_ref, x_ref, wq_ref, wk_ref, wv_ref, wo_ref, wc_ref,
+    din_ref, own_ref, other_ref, small_ref,
+    q_s, k_s, v_s, dq_s, dk_s, dv_s, p_s, cs_s, dqa_s, dka_s, dm_s,
 ):
     rows, width = x_ref.shape
     length = rows // 2
@@ -147,13 +147,23 @@
             query = jnp.where(mask, query, jnp.zeros_like(query))
             dqa_s[s * length:(s + 1) * length, first:last] += mm(d_scores, keys)
             dka_s[o * length:(o + 1) * length, first:last] += mm(d_scores, query, TN)
-    dq_ref[...] = dqa_s[...].astype(BF)
-    dk_ref[...] = dka_s[...].astype(BF)
+    dq_s[...] = dqa_s[...].astype(BF)
+    dk_s[...] = dka_s[...].astype(BF)
+
+    @pl.when(core_ref[0] == 0)
+    def _():
+        own_ref[...] = dq_s[...]
+        other_ref[...] = dk_s[...]
+
+    @pl.when(core_ref[0] == 1)
+    def _():
+        own_ref[...] = dk_s[...]
+        other_ref[...] = dq_s[...]
 
     def back(n, carry):
         sl = pl.ds(pl.multiple_of(n * step, step), step)
-        total = mm(dq_ref[...], wq_ref[sl, :], NT)
-        total = total + mm(dk_ref[...], wk_ref[sl, :], NT)
+        total = mm(dq_s[...], wq_ref[sl, :], NT)
+        total = total + mm(dk_s[...], wk_ref[sl, :], NT)
         total = total + mm(dv_s[...], wv_ref[sl, :], NT)
         for s in range(2):
             live = row_ids < lens_ref[s]
@@ -166,7 +176,7 @@
     lax.fori_loop(0, width // step, back, 0)
 
 
-def local_step(x, lens, label, wq, wk, wv, wo, wc):
+def local_step(x, lens, label, core, wq, wk, wv, wo, wc):
     rows, width = x.shape
     length = rows // 2
     vmem = pl.BlockSpec(memory_space=pltpu.VMEM)
@@ -175,9 +185,11 @@
     return pl.pallas_call(
         local_kernel,
         out_shape=(like, like, like, jax.ShapeDtypeStruct((2 * HEADS + 8, width), BF)),
-        in_specs=[smem, smem] + [vmem] * 6,
+        in_specs=[smem] * 3 + [vmem] * 6,
         out_specs=(vmem,) * 4,
         scratch_shapes=[
+            pltpu.VMEM((rows, width), BF),
+            pltpu.VMEM((rows, width), BF),
             pltpu.VMEM((rows, width), BF),
             pltpu.VMEM((rows, width), BF),
             pltpu.VMEM((rows, width), BF),
@@ -188,35 +200,33 @@
             pltpu.VMEM((rows, width), F32),
             pltpu.VMEM((8, width), F32),
         ],
-        compiler_params=pltpu.CompilerParams(vmem_limit_bytes=48 * 1024 * 1024),
+        compiler_params=pltpu.CompilerParams(vmem_limit_bytes=30 * 1024 * 1024),
         cost_estimate=pl.CostEstimate(
             flops=6 * 2 * rows * width * width,
             bytes_accessed=4 * 2 * width * width + 8 * 2 * rows * width,
             transcendentals=2 * HEADS * length * length,
         ),
-    )(lens, label, x, wq, wk, wv, wo, wc.reshape(1, width))
+    )(lens, label, core.reshape(1), x, wq, wk, wv, wo, wc.reshape(1, width))
 
 
 def swap(value, n, bit):
     return lax.ppermute(value, "dev", [(i, i ^ (1 << bit)) for i in range(n)])
 
 
-def halve(part, me, n, order):
-    bits = (n // 2).bit_length() - 1
-    cols = part.shape[-2:]
-    part = part.reshape((2,) * bits + part.shape[1:])
-    left = list(range(bits, 0, -1))
-    for turn, bit in enumerate(order):
-        axis = left.index(bit)
-        mine = (me >> bit) & 1
-        keep = lax.dynamic_index_in_dim(part, mine, axis, keepdims=False)
-        send = lax.dynamic_index_in_dim(part, 1 - mine, axis, keepdims=False)
-        got = swap(send, n, bit)
-        part = keep.astype(F32) + got.astype(F32)
-        if turn < len(order) - 1:
-            part = part.astype(BF)
-        left.pop(axis)
-    return part.reshape((2,) + cols)
+def halve_step(part, me, n, bit, left):
+    axis = left.index(bit)
+    mine = (me >> bit) & 1
+    keep = lax.dynamic_index_in_dim(part, mine, axis, keepdims=False)
+    send = lax.dynamic_index_in_dim(part, 1 - mine, axis, keepdims=False)
+    return keep, swap(send, n, bit), [b for b in left if b != bit]
+
+
+def chain_sums(by_rows, slot_ids, chain_total):
+    slots, row_block, width = by_rows.shape
+    chain_index = jnp.arange(chain_total, dtype=jnp.int32)
+    selector = (chain_index[:, None] == slot_ids[None, :]).astype(BF)
+    summed = mm(selector, by_rows.reshape(slots, row_block * width)).astype(BF)
+    return summed.reshape(chain_total, row_block, width)
 
 
 def shards(n, embeddings, lengths, pairs, labels, w_query, w_key, w_value, w_out, w_class):
@@ -232,50 +242,61 @@
     my_pair = lax.dynamic_index_in_dim(pairs, me, 0, keepdims=False)
     chain_lens = lengths.at[my_pair].get(mode="promise_in_bounds")
 
-    x_other = swap(x, n, 0)
-    d_input, d_query, d_keys, small = local_step(
-        x, chain_lens, labels, w_query, w_key, w_value, w_out, w_class
-    )
-
+    x_both = jnp.concatenate([x, swap(x, n, 0)], axis=0)
     core = me & 1
     first = core == 0
-    own = jnp.where(first, d_query, d_keys)
-    theirs = swap(jnp.where(first, d_keys, d_query), n, 0)
+    d_input, own, other, small = local_step(
+        x, chain_lens, labels, core, w_query, w_key, w_value, w_out, w_class
+    )
+    own_both = jnp.concatenate([own, swap(other, n, 0)], axis=0)
     factors = lax.all_gather(small, "dev", axis=0, tiled=False)
+    slot_grads = d_input.reshape(2, length, width)
+    by_rows = lax.all_to_all(slot_grads, "dev", split_axis=1, concat_axis=0, tiled=True)
 
     chips = n // 2
     block = width // n
     bits = chips.bit_length() - 1
-    orders = [list(range(1, bits + 1))]
-    if bits >= 4:
-        orders = [
-            [1, 2] + list(range(3, bits + 1)),
-            [2, 1] + list(range(3, bits + 1)),
-            list(range(3, bits + 1)) + [1, 2],
-        ]
-    cuts = [0, width] if len(orders) == 1 else [0, 512, 1024, width]
-    sums = []
-    for order, lo, hi in zip(orders, cuts[:-1], cuts[1:]):
-        part = mm(x, own[:, lo:hi], TN) + mm(x_other, theirs[:, lo:hi], TN)
-        part = part.astype(BF).reshape(chips, 2, block, hi - lo)
-        sums.append(halve(part, me, n, order))
-    chip_sum = jnp.concatenate(sums, axis=-1)
+    straight = list(range(1, bits + 1))
+    crossed = list(straight)
+    for i in range(0, bits - 1, 2):
+        crossed[i], crossed[i + 1] = straight[i + 1], straight[i]
+    orders = [straight, crossed]
+    half = width // 2
+    parts = [
+        mm(x_both, own_both[:, i * half:(i + 1) * half], TN)
+        .astype(BF)
+        .reshape((2,) * bits + (2, block, half))
+        for i in range(2)
+    ]
+    lefts = [straight[::-1]] * 2
+    for turn in range(bits):
+        kept, came = [], []
+        for i in range(2):
+            keep, got, lefts[i] = halve_step(parts[i], me, n, orders[i][turn], lefts[i])
+            kept.append(keep)
+            came.append(got)
+        if turn == 0:
+            came[0], came[1], by_rows = lax.optimization_barrier((came[0], came[1], by_rows))
+            summed = chain_sums(by_rows, slot_ids, chain_total)
+        elif turn == 1:
+            came[0], came[1], summed = lax.optimization_barrier((came[0], came[1], summed))
+        else:
+            came = list(lax.optimization_barrier(tuple(came)))
+        parts = [k.astype(F32) + g.astype(F32) for k, g in zip(kept, came)]
+        if turn < bits - 1:
+            parts = [part.astype(BF) for part in parts]
+    chip_sum = jnp.concatenate(parts, axis=-1)
     kept = lax.dynamic_index_in_dim(chip_sum, core, 0, keepdims=False)
     passed = lax.dynamic_index_in_dim(chip_sum, 1 - core, 0, keepdims=False)
     got = swap(passed.astype(BF), n, 0).astype(F32)
     d_wq = jnp.where(first, kept, got)
     d_wk = jnp.where(first, got, kept)
 
-    slot_grads = d_input.reshape(2, length, width)
-    by_rows = lax.all_to_all(slot_grads, "dev", split_axis=1, concat_axis=0, tiled=True)
-    row_block = by_rows.shape[1]
-    chain_index = jnp.arange(chain_total, dtype=jnp.int32)
-    selector = (chain_index[:, None] == slot_ids[None, :]).astype(BF)
-    summed = mm(selector, by_rows.reshape(slot_ids.shape[0], row_block * width)).astype(BF)
-    summed = summed.reshape(chain_total, row_block, width)
     d_embeddings = lax.all_to_all(summed, "dev", split_axis=0, concat_axis=1, tiled=True)
 
-    mine = lax.dynamic_slice_in_dim(factors, me * block, block, 2)
+    column = jnp.arange(width, dtype=jnp.int32)[:, None]
+    pick = (column == me * block + jnp.arange(block, dtype=jnp.int32)[None, :]).astype(BF)
+    mine = mm(factors.reshape(-1, width), pick).astype(BF).reshape(n, -1, block)
     tail = 2 * HEADS
     head_of = jnp.arange(width, dtype=jnp.int32) // (width // HEADS)
     own_head = head_of[None, :] == jnp.arange(HEADS, dtype=jnp.int32)[:, None]

time: 194 us -> 191 us (0.985)
  local copies, waits for them, and re-layouts: 20.9 us -> 28.3 us
  starting transfers between devices: 33 us -> 28.9 us
  Pallas kernels: 16.7 us -> 13.3 us
  matrix products: 8.72 us -> 6.53 us
    ppermute x15 -> x11, waiting for transfers between devices: 60.6 us -> 50.8 us  [swap(): return lax.ppermute(value, 'dev', [(i, i ^ 1 << bit) for i in range(n)])]
    all_to_all x1, waiting for transfers between devices: 0.01 us -> 8.14 us  [shards(): lax.all_to_all(slot_grads, 'dev', split_axis=1, concat_axis=0, tiled=True)]
    unnamed x14 -> x25, local copies, waits for them, and re-layouts: 6.34 us -> 12.3 us
    pallas_call x1, Pallas kernels: 16.7 us -> 13.3 us  [local_step(): pl.pallas_call(local_kernel, out_shape=(like, like, like, jax.ShapeDtypeS...]
    ppermute x15 -> x11, starting transfers between devices: 14.4 us -> 11.7 us  [swap(): return lax.ppermute(value, 'dev', [(i, i ^ 1 << bit) for i in range(n)])]
    dot_general x9 -> x6, matrix products: 8.72 us -> 6.53 us  [mm(): return lax.dot_general(a, b, dims, preferred_element_type=F32)]
    convert_element_type x9 -> x7, other arithmetic: 3.05 us -> 4.25 us  [the longest x6 4.23 us: shards(): parts = [part.astype(BF) for part in parts]]
  transfers between devices with their start and end apart: 20 -> 16, of which waited for: 13 -> 12; matrix products, arithmetic and copies ran while one was open for 11% -> 10% of each run, Pallas kernels for 9% -> 0%
where the time goes in v2:
time: 191 us; the launch traced here: 190 us
  waiting for transfers between devices  93.5 us (49%)
  starting transfers between devices  28.9 us (15%)
  local copies, waits for them, and re-layouts  28.3 us (15%)
  between operations  15.1 us (8%)
  Pallas kernels  13.3 us (7%)
  matrix products  6.53 us (3%)
  other arithmetic  4.78 us (3%)
    ppermute x11, waiting for transfers between devices, swap(): return lax.ppermute(value, 'dev', [(i, i ^ 1 << bit) for i in range(n)])  50.8 us
    all_to_all x1, waiting for transfers between devices, shards(): lax.all_to_all(embeddings, 'dev', split_axis=1, concat_axis=0, tiled=True)  17.7 us
    all_to_all x1, waiting for transfers between devices, shards(): lax.all_to_all(picked, 'dev', split_axis=0, concat_axis=1, tiled=True)  16.4 us
    pallas_call x1, Pallas kernels, local_step(): pl.pallas_call(local_kernel, out_shape=(like, like, like, jax.ShapeDtypeS...  13.3 us
    unnamed x25, local copies, waits for them, and re-layouts  12.3 us
    ppermute x11, starting transfers between devices, swap(): return lax.ppermute(value, 'dev', [(i, i ^ 1 << bit) for i in range(n)])  11.7 us
    all_to_all x1, waiting for transfers between devices, shards(): lax.all_to_all(slot_grads, 'dev', split_axis=1, concat_axis=0, tiled=True)  8.14 us
    all_to_all x1, starting transfers between devices, shards(): lax.all_to_all(embeddings, 'dev', split_axis=1, concat_axis=0, tiled=True)  7.3 us
  transfers between devices with their start and end apart: 16, of which 12 were waited for; matrix products, arithmetic and copies ran while one was open for 10% of the time, Pallas kernels for 0%

profile of v2, /device:TPU:0, one launch (start us, length us, event | category | flops | bytes accessed | tf_op | source)
XLA Modules:
  0.0 190.5 jit_solution(17087077626815500394)
XLA Ops:
  7.2 2.6 %copy.47 = bf16[2,128,1280]{2,0,1:T(2,128)(2,1)} copy(bf16[2,128,1280]{2,1,0:T(8,128)(2,1)} %param.9) | data formatting | bytes 1310720 | tf_op args[0]
  9.8 7.3 %all-to-all-start = ((bf16[2,128,1280]{2,0,1:T(2,128)(2,1)}), bf16[2,128,1280]{2,0,1:T(2,128)(2,1)S(1)}, u32[]{:S(2)}, u32[]{:S(2)}) async-start(bf16[2,128,1280]{2,0,1:T(2,128)(2,1)} %copy.47), calls=%async_computation | async-start | bytes 1310720 | tf_op jit(solution)/shard_map/all_to_all | solution.py:237
  17.3 17.7 %all-to-all-done = bf16[2,128,1280]{2,0,1:T(2,128)(2,1)S(1)} async-done(((bf16[2,128,1280]{2,0,1:T(2,128)(2,1)}), bf16[2,128,1280]{2,0,1:T(2,128)(2,1)S(1)}, u32[]{:S(2)}, u32[]{:S(2)}) %all-to-all-start) | async-done | bytes 655392 | tf_op jit(solution)/shard_map/all_to_all | solution.py:237
  35.3 1.9 %gather_fusion = bf16[64,4,1280]{2,1,0:T(4,128)(2,1)} fusion(bf16[64,4,1280]{2,1,0:T(4,128)(2,1)S(1)} %bitcast.112, s32[1024]{0:T(1024)S(1)} %pad_clamp_fusion.1), kind=kCustom, calls=%fused_computation | custom fusion | bytes 1310976 | tf_op jit(solution)/shard_map/gather | solution.py:239
  37.2 3.5 %all-to-all-start.1 = ((bf16[64,4,1280]{2,1,0:T(4,128)(2,1)}), bf16[64,4,1280]{2,1,0:T(4,128)(2,1)S(1)}, u32[]{:S(2)}, u32[]{:S(2)}) async-start(bf16[64,4,1280]{2,1,0:T(4,128)(2,1)} %gather_fusion), calls=%async_computation.1 | async-start | bytes 1310720 | tf_op jit(solution)/shard_map/all_to_all | solution.py:240
  41.6 0.6 gather_fusion.1
  42.3 16.4 %all-to-all-done.1 = bf16[64,4,1280]{2,1,0:T(4,128)(2,1)S(1)} async-done(((bf16[64,4,1280]{2,1,0:T(4,128)(2,1)}), bf16[64,4,1280]{2,1,0:T(4,128)(2,1)S(1)}, u32[]{:S(2)}, u32[]{:S(2)}) %all-to-all-start.1) | async-done | bytes 655392 | tf_op jit(solution)/shard_map/all_to_all | solution.py:240
  59.0 1.9 %copy-done.1 = bf16[1280,1280]{1,0:T(8,128)(2,1)S(1)} copy-done((bf16[1280,1280]{1,0:T(8,128)(2,1)S(1)}, bf16[1280,1280]{1,0:T(8,128)(2,1)}, u32[]{:S(2)}) %copy-start.1) | copy-done | bytes 3276824
  61.0 1.9 %copy-done.2 = bf16[1280,1280]{1,0:T(8,128)(2,1)S(1)} copy-done((bf16[1280,1280]{1,0:T(8,128)(2,1)S(1)}, bf16[1280,1280]{1,0:T(8,128)(2,1)}, u32[]{:S(2)}) %copy-start.2) | copy-done | bytes 3276824
  62.9 1.9 %copy-done.3 = bf16[1280,1280]{1,0:T(8,128)(2,1)S(1)} copy-done((bf16[1280,1280]{1,0:T(8,128)(2,1)S(1)}, bf16[1280,1280]{1,0:T(8,128)(2,1)}, u32[]{:S(2)}) %copy-start.3) | copy-done | bytes 3276824
  64.8 1.9 %copy-done.4 = bf16[1280,1280]{1,0:T(8,128)(2,1)S(1)} copy-done((bf16[1280,1280]{1,0:T(8,128)(2,1)S(1)}, bf16[1280,1280]{1,0:T(8,128)(2,1)}, u32[]{:S(2)}) %copy-start.4) | copy-done | bytes 3276824
  66.7 13.3 %shard_map.104 = (bf16[256,1280]{1,0:T(8,128)(2,1)S(1)}, bf16[256,1280]{1,0:T(8,128)(2,1)S(1)}, bf16[256,1280]{1,0:T(8,128)(2,1)S(1)}, bf16[40,1280]{1,0:T(8,128)(2,1)}) custom-call(s32[2]{0:T(128)S(1)} %gather_fusion.1, s32[1]{0:T(128)S(6)} %copy.82.label_ref, s32[1]{0:T(128)} %bitcast.7.core_ref, bf16[256,1280]{1,0:T(8,128)(2,1)S(1)} %reshape.154.x_ref, ...), custom_call_target="tpu_custom_call" | custom-call | flops 5033164800 | bytes 18350080 | tf_op jit(solution)/shard_map/pallas_call | solution.py:185
  80.7 1.5 copy.54
  82.2 3.5 %all-to-all-start.2 = ((bf16[2,128,1280]{2,0,1:T(2,128)(2,1)}), bf16[2,128,1280]{2,0,1:T(2,128)(2,1)S(1)}, u32[]{:S(2)}, u32[]{:S(2)}) async-start(bf16[2,128,1280]{2,0,1:T(2,128)(2,1)} %copy.54), calls=%async_computation.2 | async-start | bytes 1310720 | tf_op jit(solution)/shard_map/all_to_all | solution.py:254
  86.0 0.5 all-gather.3.cloned.1.call-update
  86.6 1.1 constant_dynamic-update-slice_fusion
  87.8 1.2 convolution_convert_fusion.1
  89.2 1.0 copy.78
  90.1 1.8 collective-permute-start.3
  91.9 1.2 convolution_convert_fusion.2
  93.3 1.0 copy.79
  94.2 1.5 collective-permute-start.2
  95.7 8.1 %all-to-all-done.2 = bf16[2,128,1280]{2,0,1:T(2,128)(2,1)S(1)} async-done(((bf16[2,128,1280]{2,0,1:T(2,128)(2,1)}), bf16[2,128,1280]{2,0,1:T(2,128)(2,1)S(1)}, u32[]{:S(2)}, u32[]{:S(2)}) %all-to-all-start.2) | async-done | bytes 655392 | tf_op jit(solution)/shard_map/all_to_all | solution.py:254
  103.8 1.1 copy.55
  104.9 10.5 %collective-permute-done.3 = bf16[2,2,2,2,40,640]{5,4,3,1,0,2:T(8,128)(2,1)S(1)} collective-permute-done((bf16[2,2,2,2,40,640]{5,4,3,1,0,2:T(8,128)(2,1)}, bf16[2,2,2,2,40,640]{5,4,3,1,0,2:T(8,128)(2,1)S(1)}, u32[]{:S(2)}, u32[]{:S(2)}) %collective-permute-start.3) | collective-permute-done | bytes 819232 | tf_op jit(solution)/shard_map/ppermute | solution.py:213
  115.4 1.7 collective-permute-done.2
  117.1 1.3 fusion
  118.4 0.8 dynamic-slice_bitcast_fusion
  119.2 1.3 collective-permute-start.5
  120.5 1.4 fusion.1
  122.0 0.8 collective-permute-start.4
  123.3 1.3 reshape.161
  124.6 5.7 %collective-permute-done.5 = bf16[2,2,2,40,640]{4,3,2,1,0:T(8,128)(2,1)} collective-permute-done((bf16[2,2,2,40,640]{4,3,2,1,0:T(8,128)(2,1)}, bf16[2,2,2,40,640]{4,3,2,1,0:T(8,128)(2,1)}, u32[]{:S(2)}, u32[]{:S(2)}) %collective-permute-start.5) | collective-permute-done | bytes 409632 | tf_op jit(solution)/shard_map/ppermute | solution.py:213
  130.4 2.3 %collective-permute-done.4 = bf16[2,2,2,40,640]{4,3,2,0,1:T(8,128)(2,1)S(1)} collective-permute-done((bf16[2,2,2,40,640]{4,3,2,0,1:T(8,128)(2,1)S(1)}, bf16[2,2,2,40,640]{4,3,2,0,1:T(8,128)(2,1)S(1)}, u32[]{:S(2)}, u32[]{:S(2)}) %collective-permute-start.4) | collective-permute-done | bytes 409632 | tf_op jit(solution)/shard_map/ppermute | solution.py:213
  132.7 1.2 fusion.2
  134.0 2.7 %collective-permute-start.7 = (bf16[2,2,40,640]{3,2,1,0:T(8,128)(2,1)S(1)}, bf16[2,2,40,640]{3,2,1,0:T(8,128)(2,1)S(1)}, u32[]{:S(2)}, u32[]{:S(2)}) collective-permute-start(bf16[2,2,40,640]{3,2,1,0:T(8,128)(2,1)S(1)} %dynamic-slice_bitcast_fusion.2), channel_id=1, source_target_pairs={{0,16},{1,17},{2,18},{3,19},{4,20},{5,21},{6,22},{7,23},{8,24},{9,... | collective-permute-start | bytes 614408 | tf_op jit(solution)/shard_map/ppermute | solution.py:213
  136.9 2.6 %all-to-all-start.3 = ((bf16[64,4,1280]{2,1,0:T(4,128)(2,1)}), bf16[64,4,1280]{2,1,0:T(4,128)(2,1)S(1)}, u32[]{:S(2)}, u32[]{:S(2)}) async-start(bf16[64,4,1280]{2,1,0:T(4,128)(2,1)} %reshape.161), calls=%async_computation.3 | async-start | bytes 1310720 | tf_op jit(solution)/shard_map/all_to_all | solution.py:295
  139.6 15.0 %collective-permute-done.7 = bf16[2,2,40,640]{3,2,1,0:T(8,128)(2,1)S(1)} collective-permute-done((bf16[2,2,40,640]{3,2,1,0:T(8,128)(2,1)S(1)}, bf16[2,2,40,640]{3,2,1,0:T(8,128)(2,1)S(1)}, u32[]{:S(2)}, u32[]{:S(2)}) %collective-permute-start.7) | collective-permute-done | bytes 204832 | tf_op jit(solution)/shard_map/ppermute | solution.py:213
  155.3 2.9 %collective-permute-start.8 = (bf16[2,40,640]{2,1,0:T(8,128)(2,1)S(1)}, bf16[2,40,640]{2,1,0:T(8,128)(2,1)S(1)}, u32[]{:S(2)}, u32[]{:S(2)}) collective-permute-start(bf16[2,40,640]{2,1,0:T(8,128)(2,1)S(1)} %dynamic-slice_bitcast_fusion.5), channel_id=1, source_target_pairs={{0,16},{1,17},{2,18},{3,19},{4,20},{5,21},{6,22},{7,23},{8,24},{9,... | collective-permute-start | bytes 307208 | tf_op jit(solution)/shard_map/ppermute | solution.py:213
  158.2 6.4 %collective-permute-done.9 = bf16[2,40,640]{2,1,0:T(8,128)(2,1)S(1)} collective-permute-done((bf16[2,40,640]{2,1,0:T(8,128)(2,1)S(1)}, bf16[2,40,640]{2,1,0:T(8,128)(2,1)S(1)}, u32[]{:S(2)}, u32[]{:S(2)}) %collective-permute-start.9) | collective-permute-done | bytes 102432 | tf_op jit(solution)/shard_map/ppermute | solution.py:213
  164.6 7.4 %collective-permute-done.8 = bf16[2,40,640]{2,1,0:T(8,128)(2,1)S(1)} collective-permute-done((bf16[2,40,640]{2,1,0:T(8,128)(2,1)S(1)}, bf16[2,40,640]{2,1,0:T(8,128)(2,1)S(1)}, u32[]{:S(2)}, u32[]{:S(2)}) %collective-permute-start.8) | collective-permute-done | bytes 102432 | tf_op jit(solution)/shard_map/ppermute | solution.py:213
  172.2 1.3 collective-permute-done.10
  173.6 1.5 reshape.167
  175.1 3.0 %convolution_convert_fusion.3 = bf16[1280,40]{0,1:T(8,128)(2,1)S(1)} fusion(bf16[1280,1280]{1,0:T(8,128)(2,1)} %all-gather.3.cloned.1.call-done, s32[40]{0:T(128)S(1)} %iota_add_fusion), kind=kOutput, calls=%fused_computation.8 | convolution fusion | flops 131174400 | bytes 3379360 | tf_op jit(solution)/shard_map/dot_general | solution.py:19
  178.2 0.6 reshape.163
  179.2 1.6 fusion.24
  181.5 0.6 convolution_bitcast_fusion.1
  182.4 1.2 copy.61
  (65 shorter events, 5.5 us)
Async XLA Ops:
  7.2 34.4 %copy-start = (s32[64]{0:T(128)S(1)}, s32[64]{0:T(128)}, u32[]{:S(2)}) copy-start(s32[64]{0:T(128)} %param.10) | copy-start | bytes 772
  7.2 9.9 %copy-start.8 = (s32[32,2]{0,1:T(2,128)S(1)}, s32[32,2]{0,1:T(2,128)}, u32[]{:S(2)}) copy-start(s32[32,2]{0,1:T(2,128)} %param.11) | copy-start | bytes 772
  9.8 25.2 %all-to-all-start = ((bf16[2,128,1280]{2,0,1:T(2,128)(2,1)}), bf16[2,128,1280]{2,0,1:T(2,128)(2,1)S(1)}, u32[]{:S(2)}, u32[]{:S(2)}) async-start(bf16[2,128,1280]{2,0,1:T(2,128)(2,1)} %copy.47), calls=%async_computation | async-start | bytes 1310720 | tf_op jit(solution)/shard_map/all_to_all | solution.py:237
  35.3 5.6 %copy-start.7 = (f32[1280]{0:T(1024)S(1)}, f32[1280]{0:T(1024)}, u32[]{:S(2)}) copy-start(f32[1280]{0:T(1024)} %param.17) | copy-start | bytes 15364
  37.2 21.4 %all-to-all-start.1 = ((bf16[64,4,1280]{2,1,0:T(4,128)(2,1)}), bf16[64,4,1280]{2,1,0:T(4,128)(2,1)S(1)}, u32[]{:S(2)}, u32[]{:S(2)}) async-start(bf16[64,4,1280]{2,1,0:T(4,128)(2,1)} %gather_fusion), calls=%async_computation.1 | async-start | bytes 1310720 | tf_op jit(solution)/shard_map/all_to_all | solution.py:240
  59.0 1.9 %copy-start.1 = (bf16[1280,1280]{1,0:T(8,128)(2,1)S(1)}, bf16[1280,1280]{1,0:T(8,128)(2,1)}, u32[]{:S(2)}) copy-start(bf16[1280,1280]{1,0:T(8,128)(2,1)} %wq_ref.1) | copy-start | bytes 9830404
  61.0 1.9 %copy-start.2 = (bf16[1280,1280]{1,0:T(8,128)(2,1)S(1)}, bf16[1280,1280]{1,0:T(8,128)(2,1)}, u32[]{:S(2)}) copy-start(bf16[1280,1280]{1,0:T(8,128)(2,1)} %wk_ref.1) | copy-start | bytes 9830404
  62.9 1.9 %copy-start.3 = (bf16[1280,1280]{1,0:T(8,128)(2,1)S(1)}, bf16[1280,1280]{1,0:T(8,128)(2,1)}, u32[]{:S(2)}) copy-start(bf16[1280,1280]{1,0:T(8,128)(2,1)} %wv_ref.1) | copy-start | bytes 9830404
  64.8 1.9 %copy-start.4 = (bf16[1280,1280]{1,0:T(8,128)(2,1)S(1)}, bf16[1280,1280]{1,0:T(8,128)(2,1)}, u32[]{:S(2)}) copy-start(bf16[1280,1280]{1,0:T(8,128)(2,1)} %wo_ref.1) | copy-start | bytes 9830404
  80.1 6.5 %collective-permute-start.1 = (bf16[256,1280]{1,0:T(8,128)(2,1)S(1)}, bf16[256,1280]{1,0:T(8,128)(2,1)S(1)}, u32[]{:S(2)}, u32[]{:S(2)}) collective-permute-start(bf16[256,1280]{1,0:T(8,128)(2,1)S(1)} %get-tuple-element.17), channel_id=1, source_target_pairs={{0,1},{1,0},{2,3},{3,2},{4,5},{5,4},{6,7},{7,6},{8,9},{9,8},{10,11... | collective-permute-start | bytes 1966088 | tf_op jit(solution)/shard_map/ppermute | solution.py:213
  80.3 6.4 %collective-permute-start = (bf16[256,1280]{1,0:T(8,128)(2,1)S(1)}, bf16[256,1280]{1,0:T(8,128)(2,1)}, u32[]{:S(2)}, u32[]{:S(2)}) collective-permute-start(bf16[256,1280]{1,0:T(8,128)(2,1)S(1)} %reshape.154.x_ref), channel_id=1, source_target_pairs={{0,1},{1,0},{2,3},{3,2},{4,5},{5,4},{6,7},{7,6},{8,9},{9,8},{10,11... | collective-permute-start | bytes 1966088 | tf_op jit(solution)/shard_map/ppermute | solution.py:213
  82.2 21.6 %all-to-all-start.2 = ((bf16[2,128,1280]{2,0,1:T(2,128)(2,1)}), bf16[2,128,1280]{2,0,1:T(2,128)(2,1)S(1)}, u32[]{:S(2)}, u32[]{:S(2)}) async-start(bf16[2,128,1280]{2,0,1:T(2,128)(2,1)} %copy.54), calls=%async_computation.2 | async-start | bytes 1310720 | tf_op jit(solution)/shard_map/all_to_all | solution.py:254
  85.7 89.4 %all-gather.3.cloned.1.call-start = ((), (), s32[]{:S(2)}) async-start(), calls=%async_computation.4 | async-start | bytes 3379200 | tf_op jit(solution)/shard_map/all_gather | solution.py:252
  90.1 25.3 %collective-permute-start.3 = (bf16[2,2,2,2,40,640]{5,4,3,1,0,2:T(8,128)(2,1)}, bf16[2,2,2,2,40,640]{5,4,3,1,0,2:T(8,128)(2,1)S(1)}, u32[]{:S(2)}, u32[]{:S(2)}) collective-permute-start(bf16[2,2,2,2,40,640]{5,4,3,1,0,2:T(8,128)(2,1)} %bitcast.101), channel_id=1, source_target_pairs={{0,4},{1,5},{2,6},{3,7},{4,0},{5,1},{6,2},{7,3},{8,12},{9,13},{10,... | collective-permute-start | bytes 2457608 | tf_op jit(solution)/shard_map/ppermute | solution.py:213
  94.2 22.8 %collective-permute-start.2 = (bf16[2,2,2,2,40,640]{5,4,3,0,1,2:T(8,128)(2,1)}, bf16[2,2,2,2,40,640]{5,4,3,0,1,2:T(8,128)(2,1)}, u32[]{:S(2)}, u32[]{:S(2)}) collective-permute-start(bf16[2,2,2,2,40,640]{5,4,3,0,1,2:T(8,128)(2,1)} %bitcast.102), channel_id=1, source_target_pairs={{0,2},{1,3},{2,0},{3,1},{4,6},{5,7},{6,4},{7,5},{8,10},{9,11},{10,... | collective-permute-start | bytes 2457608 | tf_op jit(solution)/shard_map/ppermute | solution.py:213
  115.4 1.7 copy-start.6
  119.2 11.1 %collective-permute-start.5 = (bf16[2,2,2,40,640]{4,3,2,1,0:T(8,128)(2,1)}, bf16[2,2,2,40,640]{4,3,2,1,0:T(8,128)(2,1)}, u32[]{:S(2)}, u32[]{:S(2)}) collective-permute-start(bf16[2,2,2,40,640]{4,3,2,1,0:T(8,128)(2,1)} %dynamic-slice_bitcast_fusion), channel_id=1, source_target_pairs={{0,2},{1,3},{2,0},{3,1},{4,6},{5,7},{6,4},{7,5},{8,10},{9,11},{10,... | collective-permute-start | bytes 1228808 | tf_op jit(solution)/shard_map/ppermute | solution.py:213
  120.5 2.4 %copy-start.5 = (bf16[32,2,4,1280]{3,2,1,0:T(4,128)(2,1)S(1)}, bf16[32,2,4,1280]{3,2,1,0:T(4,128)(2,1)}, u32[]{:S(2)}) copy-start(bf16[32,2,4,1280]{3,2,1,0:T(4,128)(2,1)} %copy.55) | copy-start | bytes 1966084
  122.0 10.7 %collective-permute-start.4 = (bf16[2,2,2,40,640]{4,3,2,0,1:T(8,128)(2,1)S(1)}, bf16[2,2,2,40,640]{4,3,2,0,1:T(8,128)(2,1)S(1)}, u32[]{:S(2)}, u32[]{:S(2)}) collective-permute-start(bf16[2,2,2,40,640]{4,3,2,0,1:T(8,128)(2,1)S(1)} %dynamic-slice_bitcast_fusion.1), channel_id=1, source_target_pairs={{0,4},{1,5},{2,6},{3,7},{4,0},{5,1},{6,2},{7,3},{8,12},{9,13},{10,... | collective-permute-start | bytes 1228808 | tf_op jit(solution)/shard_map/ppermute | solution.py:213
  134.0 20.6 %collective-permute-start.7 = (bf16[2,2,40,640]{3,2,1,0:T(8,128)(2,1)S(1)}, bf16[2,2,40,640]{3,2,1,0:T(8,128)(2,1)S(1)}, u32[]{:S(2)}, u32[]{:S(2)}) collective-permute-start(bf16[2,2,40,640]{3,2,1,0:T(8,128)(2,1)S(1)} %dynamic-slice_bitcast_fusion.2), channel_id=1, source_target_pairs={{0,16},{1,17},{2,18},{3,19},{4,20},{5,21},{6,22},{7,23},{8,24},{9,... | collective-permute-start | bytes 614408 | tf_op jit(solution)/shard_map/ppermute | solution.py:213
  136.8 18.2 %collective-permute-start.6 = (bf16[2,2,40,640]{3,2,1,0:T(8,128)(2,1)S(1)}, bf16[2,2,40,640]{3,2,1,0:T(8,128)(2,1)S(1)}, u32[]{:S(2)}, u32[]{:S(2)}) collective-permute-start(bf16[2,2,40,640]{3,2,1,0:T(8,128)(2,1)S(1)} %dynamic-slice_bitcast_fusion.3), channel_id=1, source_target_pairs={{0,8},{1,9},{2,10},{3,11},{4,12},{5,13},{6,14},{7,15},{8,0},{9,1},... | collective-permute-start | bytes 614408 | tf_op jit(solution)/shard_map/ppermute | solution.py:213
  136.9 36.6 %all-to-all-start.3 = ((bf16[64,4,1280]{2,1,0:T(4,128)(2,1)}), bf16[64,4,1280]{2,1,0:T(4,128)(2,1)S(1)}, u32[]{:S(2)}, u32[]{:S(2)}) async-start(bf16[64,4,1280]{2,1,0:T(4,128)(2,1)} %reshape.161), calls=%async_computation.3 | async-start | bytes 1310720 | tf_op jit(solution)/shard_map/all_to_all | solution.py:295
  155.1 9.5 %collective-permute-start.9 = (bf16[2,40,640]{2,1,0:T(8,128)(2,1)S(1)}, bf16[2,40,640]{2,1,0:T(8,128)(2,1)S(1)}, u32[]{:S(2)}, u32[]{:S(2)}) collective-permute-start(bf16[2,40,640]{2,1,0:T(8,128)(2,1)S(1)} %dynamic-slice_bitcast_fusion.4), channel_id=1, source_target_pairs={{0,8},{1,9},{2,10},{3,11},{4,12},{5,13},{6,14},{7,15},{8,0},{9,1},... | collective-permute-start | bytes 307208 | tf_op jit(solution)/shard_map/ppermute | solution.py:213
  155.3 16.8 %collective-permute-start.8 = (bf16[2,40,640]{2,1,0:T(8,128)(2,1)S(1)}, bf16[2,40,640]{2,1,0:T(8,128)(2,1)S(1)}, u32[]{:S(2)}, u32[]{:S(2)}) collective-permute-start(bf16[2,40,640]{2,1,0:T(8,128)(2,1)S(1)} %dynamic-slice_bitcast_fusion.5), channel_id=1, source_target_pairs={{0,16},{1,17},{2,18},{3,19},{4,20},{5,21},{6,22},{7,23},{8,24},{9,... | collective-permute-start | bytes 307208 | tf_op jit(solution)/shard_map/ppermute | solution.py:213
  172.1 1.4 collective-permute-start.10
Sparse Core Ops, SparseCore 0:
  89.4 66.0 all-gather.2

commit v3 on v2

--- a/solution.py
+++ b/solution.py
@@ -29,8 +29,9 @@
 
 
 def local_kernel(
-    lens_ref, label_ref, core_ref, x_ref, wq_ref, wk_ref, wv_ref, wo_ref, wc_ref,
+    lens_ref, label_ref, core_ref, x_ref, wq_hbm, wk_hbm, wv_hbm, wo_hbm, wc_ref,
     din_ref, own_ref, other_ref, small_ref,
+    wq_ref, wk_ref, wv_ref, wo_ref, w_sems,
     q_s, k_s, v_s, dq_s, dk_s, dv_s, p_s, cs_s, dqa_s, dka_s, dm_s,
 ):
     rows, width = x_ref.shape
@@ -38,16 +39,24 @@
     hd = width // HEADS
     scale = hd ** (-0.5)
     step = 256
+    sources = (wq_hbm, wk_hbm, wv_hbm, wo_hbm)
+    held = (wq_ref, wk_ref, wv_ref, wo_ref)
+    loads = [
+        pltpu.make_async_copy(source, place, w_sems.at[i])
+        for i, (source, place) in enumerate(zip(sources, held))
+    ]
+    for load in loads:
+        load.start()
     x = x_ref[...]
-
-    def project(n, carry):
-        sl = pl.ds(pl.multiple_of(n * step, step), step)
-        q_s[:, sl] = mm(x, wq_ref[:, sl]).astype(BF)
-        k_s[:, sl] = mm(x, wk_ref[:, sl]).astype(BF)
-        v_s[:, sl] = mm(x, wv_ref[:, sl]).astype(BF)
-        return carry
-
-    lax.fori_loop(0, width // step, project, 0)
+    for load, weight, result in zip(loads, held, (q_s, k_s, v_s)):
+        load.wait()
+
+        def project(n, carry, weight=weight, result=result):
+            sl = pl.ds(pl.multiple_of(n * step, step), step)
+            result[:, sl] = mm(x, weight[:, sl]).astype(BF)
+            return carry
+
+        lax.fori_loop(0, width // step, project, 0)
 
     def window(h):
         first = (h * hd) // 128 * 128
@@ -81,6 +90,7 @@
                 rounded * live, axis=0, keepdims=True
             )
 
+    loads[3].wait()
     lane16 = lax.broadcasted_iota(jnp.int32, (HEADS, width), 1)
     head16 = lax.broadcasted_iota(jnp.int32, (HEADS, width), 0)
     own16 = (lane16 >= head16 * hd) & (lane16 < head16 * hd + hd)
@@ -185,9 +195,14 @@
     return pl.pallas_call(
         local_kernel,
         out_shape=(like, like, like, jax.ShapeDtypeStruct((2 * HEADS + 8, width), BF)),
-        in_specs=[smem] * 3 + [vmem] * 6,
+        in_specs=[smem] * 3 + [vmem] + [pl.BlockSpec(memory_space=pl.ANY)] * 4 + [vmem],
         out_specs=(vmem,) * 4,
         scratch_shapes=[
+            pltpu.VMEM((width, width), BF),
+            pltpu.VMEM((width, width), BF),
+            pltpu.VMEM((width, width), BF),
+            pltpu.VMEM((width, width), BF),
+            pltpu.SemaphoreType.DMA((4,)),
             pltpu.VMEM((rows, width), BF),
             pltpu.VMEM((rows, width), BF),
             pltpu.VMEM((rows, width), BF),
@@ -200,7 +215,7 @@
             pltpu.VMEM((rows, width), F32),
             pltpu.VMEM((8, width), F32),
         ],
-        compiler_params=pltpu.CompilerParams(vmem_limit_bytes=30 * 1024 * 1024),
+        compiler_params=pltpu.CompilerParams(vmem_limit_bytes=56 * 1024 * 1024),
         cost_estimate=pl.CostEstimate(
             flops=6 * 2 * rows * width * width,
             bytes_accessed=4 * 2 * width * width + 8 * 2 * rows * width,
@@ -227,6 +242,28 @@
     selector = (chain_index[:, None] == slot_ids[None, :]).astype(BF)
     summed = mm(selector, by_rows.reshape(slots, row_block * width)).astype(BF)
     return summed.reshape(chain_total, row_block, width)
+
+
+def factor_grads(factors, me, n):
+    width = factors.shape[2]
+    block = width // n
+    tail = 2 * HEADS
+    column = jnp.arange(width, dtype=jnp.int32)[:, None]
+    pick = (column == me * block + jnp.arange(block, dtype=jnp.int32)[None, :]).astype(BF)
+    mine = mm(factors.reshape(-1, width), pick).astype(BF).reshape(n, -1, block)
+    head_of = jnp.arange(width, dtype=jnp.int32) // (width // HEADS)
+    own_head = head_of[None, :] == jnp.arange(HEADS, dtype=jnp.int32)[:, None]
+    grads = factors[:, tail + 4:tail + 6]
+    spread_grads = jnp.where(own_head, grads[:, :, None, :], jnp.zeros((), BF))
+    d_wv = mm(
+        mine[:, :tail].reshape(n * tail, block), spread_grads.reshape(n * tail, width), TN
+    )
+    d_wo = mm(
+        mine[:, tail:tail + 2].reshape(n * 2, block),
+        factors[:, tail + 2:tail + 4].reshape(n * 2, width),
+        TN,
+    )
+    return d_wv, d_wo
 
 
 def shards(n, embeddings, lengths, pairs, labels, w_query, w_key, w_value, w_out, w_class):
@@ -276,10 +313,21 @@
             kept.append(keep)
             came.append(got)
         if turn == 0:
-            came[0], came[1], by_rows = lax.optimization_barrier((came[0], came[1], by_rows))
             summed = chain_sums(by_rows, slot_ids, chain_total)
+            came[0], came[1], summed = lax.optimization_barrier((came[0], came[1], summed))
+            d_embeddings = lax.all_to_all(
+                summed, "dev", split_axis=0, concat_axis=1, tiled=True
+            )
         elif turn == 1:
-            came[0], came[1], summed = lax.optimization_barrier((came[0], came[1], summed))
+            came[0], came[1], d_embeddings = lax.optimization_barrier(
+                (came[0], came[1], d_embeddings)
+            )
+            d_embeddings = d_embeddings.astype(F32)
+            small_grads = factor_grads(factors, me, n)
+        elif turn == 2:
+            came[0], came[1], d_embeddings, small_grads = lax.optimization_barrier(
+                (came[0], came[1], d_embeddings, small_grads)
+            )
         else:
             came = list(lax.optimization_barrier(tuple(came)))
         parts = [k.astype(F32) + g.astype(F32) for k, g in zip(kept, came)]
@@ -292,26 +340,8 @@
     d_wq = jnp.where(first, kept, got)
     d_wk = jnp.where(first, got, kept)
 
-    d_embeddings = lax.all_to_all(summed, "dev", split_axis=0, concat_axis=1, tiled=True)
-
-    column = jnp.arange(width, dtype=jnp.int32)[:, None]
-    pick = (column == me * block + jnp.arange(block, dtype=jnp.int32)[None, :]).astype(BF)
-    mine = mm(factors.reshape(-1, width), pick).astype(BF).reshape(n, -1, block)
-    tail = 2 * HEADS
-    head_of = jnp.arange(width, dtype=jnp.int32) // (width // HEADS)
-    own_head = head_of[None, :] == jnp.arange(HEADS, dtype=jnp.int32)[:, None]
-    grads = factors[:, tail + 4:tail + 6]
-    spread_grads = jnp.where(own_head, grads[:, :, None, :], jnp.zeros((), BF))
-    d_wv = mm(
-        mine[:, :tail].reshape(n * tail, block), spread_grads.reshape(n * tail, width), TN
-    )
-    d_wo = mm(
-        mine[:, tail:tail + 2].reshape(n * 2, block),
-        factors[:, tail + 2:tail + 4].reshape(n * 2, width),
-        TN,
-    )
-    d_weights = jnp.stack([d_wq, d_wk, d_wv, d_wo], axis=1)
-    return (d_embeddings.astype(F32), d_weights)
+    d_weights = jnp.stack([d_wq, d_wk, small_grads[0], small_grads[1]], axis=1)
+    return (d_embeddings, d_weights)
 
 
 def solution(mesh):

time: 191 us -> 185 us (0.969)
  waiting for transfers between devices: 93.5 us -> 84.5 us
  Pallas kernels: 13.3 us -> 19.7 us
  local copies, waits for them, and re-layouts: 28.3 us -> 23.3 us
    ppermute x11, waiting for transfers between devices: 50.8 us -> 22.9 us  [swap(): return lax.ppermute(value, 'dev', [(i, i ^ 1 << bit) for i in range(n)])]
    all_to_all x1, waiting for transfers between devices: 0.01 us -> 18 us  [shards(): lax.all_to_all(summed, 'dev', split_axis=0, concat_axis=1, tiled=True)]
    unnamed x25 -> x23, local copies, waits for them, and re-layouts: 12.3 us -> 5.45 us
    pallas_call x1, Pallas kernels: 13.3 us -> 19.7 us  [local_step(): pl.pallas_call(local_kernel, out_shape=(like, like, like, jax.ShapeDtypeS...]
    all_to_all x1, waiting for transfers between devices: 8.14 us -> 10.7 us  [shards(): lax.all_to_all(slot_grads, 'dev', split_axis=1, concat_axis=0, tiled=True)]
  transfers between devices with their start and end apart: 16 -> 16, of which waited for: 12 -> 11; matrix products, arithmetic and copies ran while one was open for 10% -> 14% of each run, Pallas kernels for 0% -> 0%
where the time goes in v3:
time: 185 us; the launch traced here: 184 us
  waiting for transfers between devices  84.5 us (46%)
  starting transfers between devices  29.8 us (16%)
  local copies, waits for them, and re-layouts  23.3 us (13%)
  Pallas kernels  19.7 us (11%)
  between operations  15.1 us (8%)
  matrix products  6.53 us (4%)
  other arithmetic  5.16 us (3%)
    ppermute x11, waiting for transfers between devices, swap(): return lax.ppermute(value, 'dev', [(i, i ^ 1 << bit) for i in range(n)])  22.9 us
    pallas_call x1, Pallas kernels, local_step(): pl.pallas_call(local_kernel, out_shape=(like, like, like, jax.ShapeDtypeS...  19.7 us
    all_to_all x1, waiting for transfers between devices, shards(): lax.all_to_all(summed, 'dev', split_axis=0, concat_axis=1, tiled=True)  18 us
    all_to_all x1, waiting for transfers between devices, shards(): lax.all_to_all(embeddings, 'dev', split_axis=1, concat_axis=0, tiled=True)  17.7 us
    all_to_all x1, waiting for transfers between devices, shards(): lax.all_to_all(picked, 'dev', split_axis=0, concat_axis=1, tiled=True)  15.2 us
    ppermute x11, starting transfers between devices, swap(): return lax.ppermute(value, 'dev', [(i, i ^ 1 << bit) for i in range(n)])  11 us
    all_to_all x1, waiting for transfers between devices, shards(): lax.all_to_all(slot_grads, 'dev', split_axis=1, concat_axis=0, tiled=True)  10.7 us
    all_to_all x1, starting transfers between devices, shards(): lax.all_to_all(embeddings, 'dev', split_axis=1, concat_axis=0, tiled=True)  7.3 us
  transfers between devices with their start and end apart: 16, of which 11 were waited for; matrix products, arithmetic and copies ran while one was open for 14% of the time, Pallas kernels for 0%

profile of v3, /device:TPU:0, one launch (start us, length us, event | category | flops | bytes accessed | tf_op | source)
XLA Modules:
  0.0 184.1 jit_solution(5082024579540787242)
XLA Ops:
  7.2 2.6 %copy.47 = bf16[2,128,1280]{2,0,1:T(2,128)(2,1)} copy(bf16[2,128,1280]{2,1,0:T(8,128)(2,1)} %param.9) | data formatting | bytes 1310720 | tf_op args[0]
  9.8 7.3 %all-to-all-start = ((bf16[2,128,1280]{2,0,1:T(2,128)(2,1)}), bf16[2,128,1280]{2,0,1:T(2,128)(2,1)S(1)}, u32[]{:S(2)}, u32[]{:S(2)}) async-start(bf16[2,128,1280]{2,0,1:T(2,128)(2,1)} %copy.47), calls=%async_computation | async-start | bytes 1310720 | tf_op jit(solution)/shard_map/all_to_all | solution.py:274
  17.3 17.7 %all-to-all-done = bf16[2,128,1280]{2,0,1:T(2,128)(2,1)S(1)} async-done(((bf16[2,128,1280]{2,0,1:T(2,128)(2,1)}), bf16[2,128,1280]{2,0,1:T(2,128)(2,1)S(1)}, u32[]{:S(2)}, u32[]{:S(2)}) %all-to-all-start) | async-done | bytes 655392 | tf_op jit(solution)/shard_map/all_to_all | solution.py:274
  35.3 1.9 %gather_fusion = bf16[64,4,1280]{2,1,0:T(4,128)(2,1)} fusion(bf16[64,4,1280]{2,1,0:T(4,128)(2,1)S(1)} %bitcast.110, s32[1024]{0:T(1024)S(1)} %pad_clamp_fusion.1), kind=kCustom, calls=%fused_computation | custom fusion | bytes 1310976 | tf_op jit(solution)/shard_map/gather | solution.py:276
  37.2 3.5 %all-to-all-start.1 = ((bf16[64,4,1280]{2,1,0:T(4,128)(2,1)}), bf16[64,4,1280]{2,1,0:T(4,128)(2,1)S(1)}, u32[]{:S(2)}, u32[]{:S(2)}) async-start(bf16[64,4,1280]{2,1,0:T(4,128)(2,1)} %gather_fusion), calls=%async_computation.1 | async-start | bytes 1310720 | tf_op jit(solution)/shard_map/all_to_all | solution.py:277
  41.0 0.6 reshape.153.wc_ref
  42.3 1.2 gather_fusion.1
  43.4 15.2 %all-to-all-done.1 = bf16[64,4,1280]{2,1,0:T(4,128)(2,1)S(1)} async-done(((bf16[64,4,1280]{2,1,0:T(4,128)(2,1)}), bf16[64,4,1280]{2,1,0:T(4,128)(2,1)S(1)}, u32[]{:S(2)}, u32[]{:S(2)}) %all-to-all-start.1) | async-done | bytes 655392 | tf_op jit(solution)/shard_map/all_to_all | solution.py:277
  58.9 1.0 reshape.151.x_ref
  59.9 19.7 %shard_map.104 = (bf16[256,1280]{1,0:T(8,128)(2,1)}, bf16[256,1280]{1,0:T(8,128)(2,1)}, bf16[256,1280]{1,0:T(8,128)(2,1)}, bf16[40,1280]{1,0:T(8,128)(2,1)}) custom-call(s32[2]{0:T(128)} %gather_fusion.1, s32[1]{0:T(128)S(6)} %copy.83.label_ref, s32[1]{0:T(128)} %bitcast.7.core_ref, bf16[256,1280]{1,0:T(8,128)(2,1)} %reshape.151.x_ref, ...), custom_call_target="tpu_custom_call" | custom-call | flops 5033164800 | bytes 18350080 | tf_op jit(solution)/shard_map/pallas_call | solution.py:195
  80.1 2.6 %copy.55 = bf16[2,128,1280]{2,0,1:T(2,128)(2,1)} copy(bf16[2,128,1280]{2,1,0:T(8,128)(2,1)} %bitcast.118) | data formatting | bytes 1310720 | tf_op jit(solution)/shard_map/reshape | solution.py:290
  82.8 3.7 %all-to-all-start.2 = ((bf16[2,128,1280]{2,0,1:T(2,128)(2,1)}), bf16[2,128,1280]{2,0,1:T(2,128)(2,1)S(1)}, u32[]{:S(2)}, u32[]{:S(2)}) async-start(bf16[2,128,1280]{2,0,1:T(2,128)(2,1)} %copy.55), calls=%async_computation.2 | async-start | bytes 1310720 | tf_op jit(solution)/shard_map/all_to_all | solution.py:291
  86.7 1.1 constant_dynamic-update-slice_fusion
  87.8 1.2 convolution_convert_fusion.1
  89.2 1.0 copy.78
  90.1 1.6 collective-permute-start.3
  91.7 1.2 convolution_convert_fusion.2
  93.1 1.0 copy.79
  94.1 1.5 collective-permute-start.2
  95.7 10.7 %all-to-all-done.2 = bf16[2,128,1280]{2,0,1:T(2,128)(2,1)S(1)} async-done(((bf16[2,128,1280]{2,0,1:T(2,128)(2,1)}), bf16[2,128,1280]{2,0,1:T(2,128)(2,1)S(1)}, u32[]{:S(2)}, u32[]{:S(2)}) %all-to-all-start.2) | async-done | bytes 655392 | tf_op jit(solution)/shard_map/all_to_all | solution.py:291
  107.1 1.3 reshape.158
  108.4 8.2 %collective-permute-done.3 = bf16[2,2,2,2,40,640]{5,4,3,1,0,2:T(8,128)(2,1)} collective-permute-done((bf16[2,2,2,2,40,640]{5,4,3,1,0,2:T(8,128)(2,1)}, bf16[2,2,2,2,40,640]{5,4,3,1,0,2:T(8,128)(2,1)}, u32[]{:S(2)}, u32[]{:S(2)}) %collective-permute-start.3) | collective-permute-done | bytes 819232 | tf_op jit(solution)/shard_map/ppermute | solution.py:228
  116.6 2.8 %collective-permute-done.2 = bf16[2,2,2,2,40,640]{5,4,3,0,1,2:T(8,128)(2,1)S(1)} collective-permute-done((bf16[2,2,2,2,40,640]{5,4,3,0,1,2:T(8,128)(2,1)}, bf16[2,2,2,2,40,640]{5,4,3,0,1,2:T(8,128)(2,1)S(1)}, u32[]{:S(2)}, u32[]{:S(2)}) %collective-permute-start.2) | collective-permute-done | bytes 819232 | tf_op jit(solution)/shard_map/ppermute | solution.py:228
  119.5 0.9 copy-done.2
  120.4 4.3 %all-to-all-start.3 = ((bf16[64,4,1280]{2,1,0:T(4,128)(2,1)}), bf16[64,4,1280]{2,1,0:T(4,128)(2,1)S(1)}, u32[]{:S(2)}, u32[]{:S(2)}) async-start(bf16[64,4,1280]{2,1,0:T(4,128)(2,1)} %reshape.158), calls=%async_computation.3 | async-start | bytes 1310720 | tf_op jit(solution)/shard_map/all_to_all | solution.py:318
  124.6 0.5 iota_add_fusion
  125.2 1.5 fusion
  126.7 0.8 dynamic-slice_bitcast_fusion
  127.5 1.7 collective-permute-start.5
  129.4 0.8 dynamic-slice_bitcast_fusion.1
  130.2 1.5 collective-permute-start.4
  131.7 18.0 %all-to-all-done.3 = bf16[64,4,1280]{2,1,0:T(4,128)(2,1)S(1)} async-done(((bf16[64,4,1280]{2,1,0:T(4,128)(2,1)}), bf16[64,4,1280]{2,1,0:T(4,128)(2,1)S(1)}, u32[]{:S(2)}, u32[]{:S(2)}) %all-to-all-start.3) | async-done | bytes 655392 | tf_op jit(solution)/shard_map/all_to_all | solution.py:318
  150.0 1.1 fusion.2
  151.2 1.6 collective-permute-start.7
  152.8 1.1 convert_element_type.135
  154.1 1.6 collective-permute-start.6
  155.7 3.0 %convolution_convert_fusion.3 = bf16[1280,40]{0,1:T(8,128)(2,1)S(1)} fusion(bf16[1280,1280]{1,0:T(8,128)(2,1)} %all-gather.3.cloned.1.call-done, s32[40]{0:T(128)S(1)} %copy-done.7), kind=kOutput, calls=%fused_computation.7 | convolution fusion | flops 131174400 | bytes 3379360 | tf_op jit(solution)/shard_map/dot_general | solution.py:19
  158.7 0.6 reshape.160
  159.6 1.6 fusion.24
  161.5 0.6 fusion.25
  162.2 0.5 copy.64
  162.9 1.1 collective-permute-done.7
  164.0 1.9 %collective-permute-done.6 = bf16[2,2,40,640]{3,2,1,0:T(8,128)(2,1)S(1)} collective-permute-done((bf16[2,2,40,640]{3,2,1,0:T(8,128)(2,1)S(1)}, bf16[2,2,40,640]{3,2,1,0:T(8,128)(2,1)S(1)}, u32[]{:S(2)}, u32[]{:S(2)}) %collective-permute-start.6) | collective-permute-done | bytes 204832 | tf_op jit(solution)/shard_map/ppermute | solution.py:228
  166.1 0.9 collective-permute-start.8
  167.0 5.4 %collective-permute-done.9 = bf16[2,40,640]{2,1,0:T(8,128)(2,1)S(1)} collective-permute-done((bf16[2,40,640]{2,1,0:T(8,128)(2,1)S(1)}, bf16[2,40,640]{2,1,0:T(8,128)(2,1)S(1)}, u32[]{:S(2)}, u32[]{:S(2)}) %collective-permute-start.9) | collective-permute-done | bytes 102432 | tf_op jit(solution)/shard_map/ppermute | solution.py:228
  172.4 2.1 %collective-permute-done.8 = bf16[2,40,640]{2,1,0:T(8,128)(2,1)S(1)} collective-permute-done((bf16[2,40,640]{2,1,0:T(8,128)(2,1)S(1)}, bf16[2,40,640]{2,1,0:T(8,128)(2,1)S(1)}, u32[]{:S(2)}, u32[]{:S(2)}) %collective-permute-start.8) | collective-permute-done | bytes 102432 | tf_op jit(solution)/shard_map/ppermute | solution.py:228
  174.6 1.3 collective-permute-done.10
  176.0 1.2 copy.61
  (64 shorter events, 4.9 us)
Async XLA Ops:
  7.2 35.1 %copy-start = (s32[64]{0:T(128)S(1)}, s32[64]{0:T(128)}, u32[]{:S(2)}) copy-start(s32[64]{0:T(128)} %param.10) | copy-start | bytes 772
  7.2 9.9 %copy-start.6 = (s32[32,2]{0,1:T(2,128)S(1)}, s32[32,2]{0,1:T(2,128)}, u32[]{:S(2)}) copy-start(s32[32,2]{0,1:T(2,128)} %param.11) | copy-start | bytes 772
  9.8 25.2 %all-to-all-start = ((bf16[2,128,1280]{2,0,1:T(2,128)(2,1)}), bf16[2,128,1280]{2,0,1:T(2,128)(2,1)S(1)}, u32[]{:S(2)}, u32[]{:S(2)}) async-start(bf16[2,128,1280]{2,0,1:T(2,128)(2,1)} %copy.47), calls=%async_computation | async-start | bytes 1310720 | tf_op jit(solution)/shard_map/all_to_all | solution.py:274
  35.3 5.7 %copy-start.5 = (f32[1280]{0:T(1024)S(1)}, f32[1280]{0:T(1024)}, u32[]{:S(2)}) copy-start(f32[1280]{0:T(1024)} %param.17) | copy-start | bytes 15364
  37.2 21.4 %all-to-all-start.1 = ((bf16[64,4,1280]{2,1,0:T(4,128)(2,1)}), bf16[64,4,1280]{2,1,0:T(4,128)(2,1)S(1)}, u32[]{:S(2)}, u32[]{:S(2)}) async-start(bf16[64,4,1280]{2,1,0:T(4,128)(2,1)} %gather_fusion), calls=%async_computation.1 | async-start | bytes 1310720 | tf_op jit(solution)/shard_map/all_to_all | solution.py:277
  40.7 115.0 %all-gather.3.cloned.1.call-start = ((), (), s32[]{:S(2)}) async-start(), calls=%async_computation.4 | async-start | bytes 3379200 | tf_op jit(solution)/shard_map/all_gather | solution.py:289
  59.9 19.9 %copy-start.1 = (bf16[256,1280]{1,0:T(8,128)(2,1)S(1)}, bf16[256,1280]{1,0:T(8,128)(2,1)}, u32[]{:S(2)}) copy-start(bf16[256,1280]{1,0:T(8,128)(2,1)} %reshape.151.x_ref) | copy-start | bytes 1966084
  79.6 7.0 %collective-permute-start.1 = (bf16[256,1280]{1,0:T(8,128)(2,1)}, bf16[256,1280]{1,0:T(8,128)(2,1)S(1)}, u32[]{:S(2)}, u32[]{:S(2)}) collective-permute-start(bf16[256,1280]{1,0:T(8,128)(2,1)} %get-tuple-element.20), channel_id=1, source_target_pairs={{0,1},{1,0},{2,3},{3,2},{4,5},{5,4},{6,7},{7,6},{8,9},{9,8},{10,11... | collective-permute-start | bytes 1966088 | tf_op jit(solution)/shard_map/ppermute | solution.py:228
  79.8 6.9 %collective-permute-start = (bf16[256,1280]{1,0:T(8,128)(2,1)S(1)}, bf16[256,1280]{1,0:T(8,128)(2,1)}, u32[]{:S(2)}, u32[]{:S(2)}) collective-permute-start(bf16[256,1280]{1,0:T(8,128)(2,1)S(1)} %copy-done.1), channel_id=1, source_target_pairs={{0,1},{1,0},{2,3},{3,2},{4,5},{5,4},{6,7},{7,6},{8,9},{9,8},{10,11... | collective-permute-start | bytes 1966088 | tf_op jit(solution)/shard_map/ppermute | solution.py:228
  82.8 3.8 %copy-start.4 = (bf16[256,1280]{1,0:T(8,128)(2,1)S(1)}, bf16[256,1280]{1,0:T(8,128)(2,1)}, u32[]{:S(2)}) copy-start(bf16[256,1280]{1,0:T(8,128)(2,1)} %get-tuple-element.19) | copy-start | bytes 1966084
  82.8 23.6 %all-to-all-start.2 = ((bf16[2,128,1280]{2,0,1:T(2,128)(2,1)}), bf16[2,128,1280]{2,0,1:T(2,128)(2,1)S(1)}, u32[]{:S(2)}, u32[]{:S(2)}) async-start(bf16[2,128,1280]{2,0,1:T(2,128)(2,1)} %copy.55), calls=%async_computation.2 | async-start | bytes 1310720 | tf_op jit(solution)/shard_map/all_to_all | solution.py:291
  90.1 26.5 %collective-permute-start.3 = (bf16[2,2,2,2,40,640]{5,4,3,1,0,2:T(8,128)(2,1)}, bf16[2,2,2,2,40,640]{5,4,3,1,0,2:T(8,128)(2,1)}, u32[]{:S(2)}, u32[]{:S(2)}) collective-permute-start(bf16[2,2,2,2,40,640]{5,4,3,1,0,2:T(8,128)(2,1)} %bitcast.99), channel_id=1, source_target_pairs={{0,4},{1,5},{2,6},{3,7},{4,0},{5,1},{6,2},{7,3},{8,12},{9,13},{10,... | collective-permute-start | bytes 2457608 | tf_op jit(solution)/shard_map/ppermute | solution.py:228
  94.1 25.4 %collective-permute-start.2 = (bf16[2,2,2,2,40,640]{5,4,3,0,1,2:T(8,128)(2,1)}, bf16[2,2,2,2,40,640]{5,4,3,0,1,2:T(8,128)(2,1)S(1)}, u32[]{:S(2)}, u32[]{:S(2)}) collective-permute-start(bf16[2,2,2,2,40,640]{5,4,3,0,1,2:T(8,128)(2,1)} %bitcast.100), channel_id=1, source_target_pairs={{0,2},{1,3},{2,0},{3,1},{4,6},{5,7},{6,4},{7,5},{8,10},{9,11},{10,... | collective-permute-start | bytes 2457608 | tf_op jit(solution)/shard_map/ppermute | solution.py:228
  119.5 0.9 copy-start.2
  120.4 29.3 %all-to-all-start.3 = ((bf16[64,4,1280]{2,1,0:T(4,128)(2,1)}), bf16[64,4,1280]{2,1,0:T(4,128)(2,1)S(1)}, u32[]{:S(2)}, u32[]{:S(2)}) async-start(bf16[64,4,1280]{2,1,0:T(4,128)(2,1)} %reshape.158), calls=%async_computation.3 | async-start | bytes 1310720 | tf_op jit(solution)/shard_map/all_to_all | solution.py:318
  125.2 4.0 %copy-start.3 = (bf16[2,2,2,2,40,640]{5,4,3,0,1,2:T(8,128)(2,1)S(1)}, bf16[2,2,2,2,40,640]{5,4,3,0,1,2:T(8,128)(2,1)}, u32[]{:S(2)}) copy-start(bf16[2,2,2,2,40,640]{5,4,3,0,1,2:T(8,128)(2,1)} %copy-done.2) | copy-start | bytes 2457604
  127.5 22.6 %collective-permute-start.5 = (bf16[2,2,2,40,640]{4,3,2,1,0:T(8,128)(2,1)}, bf16[2,2,2,40,640]{4,3,2,1,0:T(8,128)(2,1)}, u32[]{:S(2)}, u32[]{:S(2)}) collective-permute-start(bf16[2,2,2,40,640]{4,3,2,1,0:T(8,128)(2,1)} %dynamic-slice_bitcast_fusion), channel_id=1, source_target_pairs={{0,2},{1,3},{2,0},{3,1},{4,6},{5,7},{6,4},{7,5},{8,10},{9,11},{10,... | collective-permute-start | bytes 1228808 | tf_op jit(solution)/shard_map/ppermute | solution.py:228
  130.2 19.8 %collective-permute-start.4 = (bf16[2,2,2,40,640]{4,3,2,0,1:T(8,128)(2,1)}, bf16[2,2,2,40,640]{4,3,2,0,1:T(8,128)(2,1)S(1)}, u32[]{:S(2)}, u32[]{:S(2)}) collective-permute-start(bf16[2,2,2,40,640]{4,3,2,0,1:T(8,128)(2,1)} %dynamic-slice_bitcast_fusion.1), channel_id=1, source_target_pairs={{0,4},{1,5},{2,6},{3,7},{4,0},{5,1},{6,2},{7,3},{8,12},{9,13},{10,... | collective-permute-start | bytes 1228808 | tf_op jit(solution)/shard_map/ppermute | solution.py:228
  151.2 4.5 %copy-start.7 = (s32[40]{0:T(128)S(1)}, s32[40]{0:T(128)}, u32[]{:S(2)}) copy-start(s32[40]{0:T(128)} %iota_add_fusion) | copy-start | bytes 484
  151.2 12.8 %collective-permute-start.7 = (bf16[2,2,40,640]{3,2,1,0:T(8,128)(2,1)S(1)}, bf16[2,2,40,640]{3,2,1,0:T(8,128)(2,1)S(1)}, u32[]{:S(2)}, u32[]{:S(2)}) collective-permute-start(bf16[2,2,40,640]{3,2,1,0:T(8,128)(2,1)S(1)} %dynamic-slice_bitcast_fusion.2), channel_id=1, source_target_pairs={{0,16},{1,17},{2,18},{3,19},{4,20},{5,21},{6,22},{7,23},{8,24},{9,... | collective-permute-start | bytes 614408 | tf_op jit(solution)/shard_map/ppermute | solution.py:228
  154.1 11.8 %collective-permute-start.6 = (bf16[2,2,40,640]{3,2,1,0:T(8,128)(2,1)S(1)}, bf16[2,2,40,640]{3,2,1,0:T(8,128)(2,1)S(1)}, u32[]{:S(2)}, u32[]{:S(2)}) collective-permute-start(bf16[2,2,40,640]{3,2,1,0:T(8,128)(2,1)S(1)} %dynamic-slice_bitcast_fusion.3), channel_id=1, source_target_pairs={{0,8},{1,9},{2,10},{3,11},{4,12},{5,13},{6,14},{7,15},{8,0},{9,1},... | collective-permute-start | bytes 614408 | tf_op jit(solution)/shard_map/ppermute | solution.py:228
  165.9 6.4 %collective-permute-start.9 = (bf16[2,40,640]{2,1,0:T(8,128)(2,1)S(1)}, bf16[2,40,640]{2,1,0:T(8,128)(2,1)S(1)}, u32[]{:S(2)}, u32[]{:S(2)}) collective-permute-start(bf16[2,40,640]{2,1,0:T(8,128)(2,1)S(1)} %dynamic-slice_bitcast_fusion.4), channel_id=1, source_target_pairs={{0,8},{1,9},{2,10},{3,11},{4,12},{5,13},{6,14},{7,15},{8,0},{9,1},... | collective-permute-start | bytes 307208 | tf_op jit(solution)/shard_map/ppermute | solution.py:228
  166.1 8.4 %collective-permute-start.8 = (bf16[2,40,640]{2,1,0:T(8,128)(2,1)S(1)}, bf16[2,40,640]{2,1,0:T(8,128)(2,1)S(1)}, u32[]{:S(2)}, u32[]{:S(2)}) collective-permute-start(bf16[2,40,640]{2,1,0:T(8,128)(2,1)S(1)} %dynamic-slice_bitcast_fusion.5), channel_id=1, source_target_pairs={{0,16},{1,17},{2,18},{3,19},{4,20},{5,21},{6,22},{7,23},{8,24},{9,... | collective-permute-start | bytes 307208 | tf_op jit(solution)/shard_map/ppermute | solution.py:228
  174.6 1.4 collective-permute-start.10
Sparse Core Ops, SparseCore 0:
  79.7 73.2 all-gather.2

commit v4 on v3

--- a/solution.py
+++ b/solution.py
@@ -41,22 +41,38 @@
     step = 256
     sources = (wq_hbm, wk_hbm, wv_hbm, wo_hbm)
     held = (wq_ref, wk_ref, wv_ref, wo_ref)
-    loads = [
-        pltpu.make_async_copy(source, place, w_sems.at[i])
-        for i, (source, place) in enumerate(zip(sources, held))
-    ]
-    for load in loads:
-        load.start()
-    x = x_ref[...]
-    for load, weight, result in zip(loads, held, (q_s, k_s, v_s)):
-        load.wait()
-
-        def project(n, carry, weight=weight, result=result):
+    cut = width // 2
+
+    def start_load(i):
+        for j in range(2):
+            rows_of = pl.ds(j * cut, cut)
+            pltpu.make_async_copy(
+                sources[i].at[rows_of], held[i].at[rows_of], w_sems.at[2 * i + j]
+            ).start()
+
+    def wait_load(i):
+        for j in range(2):
+            rows_of = pl.ds(j * cut, cut)
+            pltpu.make_async_copy(
+                sources[i].at[rows_of], held[i].at[rows_of], w_sems.at[2 * i + j]
+            ).wait()
+
+    def project(weight, result):
+        def body(n, carry):
             sl = pl.ds(pl.multiple_of(n * step, step), step)
-            result[:, sl] = mm(x, weight[:, sl]).astype(BF)
+            result[:, sl] = mm(x_ref[...], weight[:, sl]).astype(BF)
             return carry
 
-        lax.fori_loop(0, width // step, project, 0)
+        lax.fori_loop(0, width // step, body, 0)
+
+    start_load(0)
+    start_load(1)
+    wait_load(0)
+    project(wq_ref, q_s)
+    wait_load(1)
+    start_load(2)
+    start_load(3)
+    project(wk_ref, k_s)
 
     def window(h):
         first = (h * hd) // 128 * 128
@@ -90,7 +106,9 @@
                 rounded * live, axis=0, keepdims=True
             )
 
-    loads[3].wait()
+    wait_load(2)
+    project(wv_ref, v_s)
+    wait_load(3)
     lane16 = lax.broadcasted_iota(jnp.int32, (HEADS, width), 1)
     head16 = lax.broadcasted_iota(jnp.int32, (HEADS, width), 0)
     own16 = (lane16 >= head16 * hd) & (lane16 < head16 * hd + hd)
@@ -202,7 +220,7 @@
             pltpu.VMEM((width, width), BF),
             pltpu.VMEM((width, width), BF),
             pltpu.VMEM((width, width), BF),
-            pltpu.SemaphoreType.DMA((4,)),
+            pltpu.SemaphoreType.DMA((8,)),
             pltpu.VMEM((rows, width), BF),
             pltpu.VMEM((rows, width), BF),
             pltpu.VMEM((rows, width), BF),
@@ -314,15 +332,17 @@
             came.append(got)
         if turn == 0:
             summed = chain_sums(by_rows, slot_ids, chain_total)
-            came[0], came[1], summed = lax.optimization_barrier((came[0], came[1], summed))
             d_embeddings = lax.all_to_all(
                 summed, "dev", split_axis=0, concat_axis=1, tiled=True
             )
+            came[0], came[1], d_embeddings = lax.optimization_barrier(
+                (came[0], came[1], d_embeddings)
+            )
+            d_embeddings = d_embeddings.astype(F32)
         elif turn == 1:
             came[0], came[1], d_embeddings = lax.optimization_barrier(
                 (came[0], came[1], d_embeddings)
             )
-            d_embeddings = d_embeddings.astype(F32)
             small_grads = factor_grads(factors, me, n)
         elif turn == 2:
             came[0], came[1], d_embeddings, small_grads = lax.optimization_barrier(

time: 185 us -> 192 us (1.038)
  waiting for transfers between devices: 84.5 us -> 92.3 us
  local copies, waits for them, and re-layouts: 23.3 us -> 20.2 us
  starting transfers between devices: 29.8 us -> 31.8 us
    all_to_all x1, waiting for transfers between devices: 10.7 us -> 15.6 us  [shards(): lax.all_to_all(slot_grads, 'dev', split_axis=1, concat_axis=0, tiled=True)]
    ppermute x11, waiting for transfers between devices: 22.9 us -> 25.7 us  [swap(): return lax.ppermute(value, 'dev', [(i, i ^ 1 << bit) for i in range(n)])]
    ppermute x11, starting transfers between devices: 11 us -> 13.8 us  [swap(): return lax.ppermute(value, 'dev', [(i, i ^ 1 << bit) for i in range(n)])]
    unnamed x23 -> x21, local copies, waits for them, and re-layouts: 5.45 us -> 4.73 us
  transfers between devices with their start and end apart: 16 -> 16, of which waited for: 11 -> 10; matrix products, arithmetic and copies ran while one was open for 14% -> 13% of each run, Pallas kernels for 0% -> 0%
where the time goes in v4:
time: 192 us
  waiting for transfers between devices  92.3 us (48%)
  starting transfers between devices  31.8 us (17%)
  local copies, waits for them, and re-layouts  20.2 us (11%)
  Pallas kernels  19.6 us (10%)
  between operations  15.1 us (8%)
  matrix products  8.02 us (4%)
  other arithmetic  4.64 us (2%)
    ppermute x11, waiting for transfers between devices, swap(): return lax.ppermute(value, 'dev', [(i, i ^ 1 << bit) for i in range(n)])  25.7 us
    pallas_call x1, Pallas kernels, local_step(): pl.pallas_call(local_kernel, out_shape=(like, like, like, jax.ShapeDtypeS...  19.6 us
    all_to_all x1, waiting for transfers between devices, shards(): lax.all_to_all(summed, 'dev', split_axis=0, concat_axis=1, tiled=True)  18.2 us
    all_to_all x1, waiting for transfers between devices, shards(): lax.all_to_all(embeddings, 'dev', split_axis=1, concat_axis=0, tiled=True)  17.7 us
    all_to_all x1, waiting for transfers between devices, shards(): lax.all_to_all(slot_grads, 'dev', split_axis=1, concat_axis=0, tiled=True)  15.6 us
    all_to_all x1, waiting for transfers between devices, shards(): lax.all_to_all(picked, 'dev', split_axis=0, concat_axis=1, tiled=True)  15.2 us
    ppermute x11, starting transfers between devices, swap(): return lax.ppermute(value, 'dev', [(i, i ^ 1 << bit) for i in range(n)])  13.8 us
    dot_general x6, matrix products, mm(): return lax.dot_general(a, b, dims, preferred_element_type=F32)  8.02 us
  transfers between devices with their start and end apart: 16, of which 10 were waited for; matrix products, arithmetic and copies ran while one was open for 13% of the time, Pallas kernels for 0%

profile of v4, /device:TPU:0, one launch (start us, length us, event | category | flops | bytes accessed | tf_op | source)
XLA Modules:
  0.0 191.7 jit_solution(918603769160626994)
XLA Ops:
  7.2 2.6 %copy.47 = bf16[2,128,1280]{2,0,1:T(2,128)(2,1)} copy(bf16[2,128,1280]{2,1,0:T(8,128)(2,1)} %param.9) | data formatting | bytes 1310720 | tf_op args[0]
  9.8 7.3 %all-to-all-start = ((bf16[2,128,1280]{2,0,1:T(2,128)(2,1)}), bf16[2,128,1280]{2,0,1:T(2,128)(2,1)S(1)}, u32[]{:S(2)}, u32[]{:S(2)}) async-start(bf16[2,128,1280]{2,0,1:T(2,128)(2,1)} %copy.47), calls=%async_computation | async-start | bytes 1310720 | tf_op jit(solution)/shard_map/all_to_all | solution.py:292
  17.3 17.7 %all-to-all-done = bf16[2,128,1280]{2,0,1:T(2,128)(2,1)S(1)} async-done(((bf16[2,128,1280]{2,0,1:T(2,128)(2,1)}), bf16[2,128,1280]{2,0,1:T(2,128)(2,1)S(1)}, u32[]{:S(2)}, u32[]{:S(2)}) %all-to-all-start) | async-done | bytes 655392 | tf_op jit(solution)/shard_map/all_to_all | solution.py:292
  35.0 0.3 copy.48
  35.3 1.9 gather_fusion
  37.2 3.5 %all-to-all-start.1 = ((bf16[64,4,1280]{2,1,0:T(4,128)(2,1)}), bf16[64,4,1280]{2,1,0:T(4,128)(2,1)S(1)}, u32[]{:S(2)}, u32[]{:S(2)}) async-start(bf16[64,4,1280]{2,1,0:T(4,128)(2,1)} %gather_fusion), calls=%async_computation.1 | async-start | bytes 1310720 | tf_op jit(solution)/shard_map/all_to_all | solution.py:295
  41.0 0.6 reshape.153.wc_ref
  42.3 1.2 gather_fusion.1
  43.5 15.2 %all-to-all-done.1 = bf16[64,4,1280]{2,1,0:T(4,128)(2,1)S(1)} async-done(((bf16[64,4,1280]{2,1,0:T(4,128)(2,1)}), bf16[64,4,1280]{2,1,0:T(4,128)(2,1)S(1)}, u32[]{:S(2)}, u32[]{:S(2)}) %all-to-all-start.1) | async-done | bytes 655392 | tf_op jit(solution)/shard_map/all_to_all | solution.py:295
  58.9 1.0 reshape.151.x_ref
  59.9 19.6 %shard_map.104 = (bf16[256,1280]{1,0:T(8,128)(2,1)}, bf16[256,1280]{1,0:T(8,128)(2,1)}, bf16[256,1280]{1,0:T(8,128)(2,1)}, bf16[40,1280]{1,0:T(8,128)(2,1)}) custom-call(s32[2]{0:T(128)} %gather_fusion.1, s32[1]{0:T(128)S(6)} %copy.83.label_ref, s32[1]{0:T(128)} %bitcast.7.core_ref, bf16[256,1280]{1,0:T(8,128)(2,1)} %reshape.151.x_ref, ...), custom_call_target="tpu_custom_call" | custom-call | flops 5033164800 | bytes 18350080 | tf_op jit(solution)/shard_map/pallas_call | solution.py:213
  79.8 0.5 collective-permute-start
  80.3 2.6 %copy.55 = bf16[2,128,1280]{2,0,1:T(2,128)(2,1)} copy(bf16[2,128,1280]{2,1,0:T(8,128)(2,1)} %bitcast.118) | data formatting | bytes 1310720 | tf_op jit(solution)/shard_map/reshape | solution.py:308
  82.9 3.7 %all-to-all-start.2 = ((bf16[2,128,1280]{2,0,1:T(2,128)(2,1)}), bf16[2,128,1280]{2,0,1:T(2,128)(2,1)S(1)}, u32[]{:S(2)}, u32[]{:S(2)}) async-start(bf16[2,128,1280]{2,0,1:T(2,128)(2,1)} %copy.55), calls=%async_computation.2 | async-start | bytes 1310720 | tf_op jit(solution)/shard_map/all_to_all | solution.py:309
  86.9 1.2 convolution_convert_fusion.1
  88.4 1.0 copy.78
  89.4 1.6 collective-permute-start.3
  91.0 15.6 %all-to-all-done.2 = bf16[2,128,1280]{2,0,1:T(2,128)(2,1)S(1)} async-done(((bf16[2,128,1280]{2,0,1:T(2,128)(2,1)}), bf16[2,128,1280]{2,0,1:T(2,128)(2,1)S(1)}, u32[]{:S(2)}, u32[]{:S(2)}) %all-to-all-start.2) | async-done | bytes 655392 | tf_op jit(solution)/shard_map/all_to_all | solution.py:309
  106.6 0.3 copy.56
  107.0 0.3 convolution_convert_fusion
  107.3 1.3 reshape.158
  108.6 3.4 %all-to-all-start.3 = ((bf16[64,4,1280]{2,1,0:T(4,128)(2,1)}), bf16[64,4,1280]{2,1,0:T(4,128)(2,1)S(1)}, u32[]{:S(2)}, u32[]{:S(2)}) async-start(bf16[64,4,1280]{2,1,0:T(4,128)(2,1)} %reshape.158), calls=%async_computation.3 | async-start | bytes 1310720 | tf_op jit(solution)/shard_map/all_to_all | solution.py:335
  112.0 2.7 %convolution_convert_fusion.2 = bf16[1280,640]{1,0:T(8,128)(2,1)S(1)} fusion(bf16[512,1280]{1,0:T(8,128)(2,1)} %copy-done.3, bf16[512,1280]{1,0:T(8,128)(2,1)} %copy-done.4), kind=kOutput, calls=%fused_computation.4 | convolution fusion | flops 839680000 | bytes 3604480 | tf_op jit(solution)/shard_map/dot_general | solution.py:19
  114.9 1.0 copy.79
  115.9 1.8 collective-permute-start.2
  117.7 18.2 %all-to-all-done.3 = bf16[64,4,1280]{2,1,0:T(4,128)(2,1)S(1)} async-done(((bf16[64,4,1280]{2,1,0:T(4,128)(2,1)}), bf16[64,4,1280]{2,1,0:T(4,128)(2,1)S(1)}, u32[]{:S(2)}, u32[]{:S(2)}) %all-to-all-start.3) | async-done | bytes 655392 | tf_op jit(solution)/shard_map/all_to_all | solution.py:335
  136.2 10.8 %collective-permute-done.2 = bf16[2,2,2,2,40,640]{5,4,3,0,1,2:T(8,128)(2,1)} collective-permute-done((bf16[2,2,2,2,40,640]{5,4,3,0,1,2:T(8,128)(2,1)}, bf16[2,2,2,2,40,640]{5,4,3,0,1,2:T(8,128)(2,1)}, u32[]{:S(2)}, u32[]{:S(2)}) %collective-permute-start.2) | collective-permute-done | bytes 819232 | tf_op jit(solution)/shard_map/ppermute | solution.py:246
  147.0 1.3 fusion
  148.4 1.1 collective-permute-start.5
  149.5 1.3 fusion.1
  150.9 1.2 collective-permute-start.4
  152.1 1.1 convert_element_type.129
  153.2 6.5 %collective-permute-done.5 = bf16[2,2,2,40,640]{4,3,2,1,0:T(8,128)(2,1)S(1)} collective-permute-done((bf16[2,2,2,40,640]{4,3,2,1,0:T(8,128)(2,1)S(1)}, bf16[2,2,2,40,640]{4,3,2,1,0:T(8,128)(2,1)S(1)}, u32[]{:S(2)}, u32[]{:S(2)}) %collective-permute-start.5) | collective-permute-done | bytes 409632 | tf_op jit(solution)/shard_map/ppermute | solution.py:246
  159.7 1.9 collective-permute-done.4
  161.8 2.5 %collective-permute-start.7 = (bf16[2,2,40,640]{3,2,1,0:T(8,128)(2,1)S(1)}, bf16[2,2,40,640]{3,2,1,0:T(8,128)(2,1)S(1)}, u32[]{:S(2)}, u32[]{:S(2)}) collective-permute-start(bf16[2,2,40,640]{3,2,1,0:T(8,128)(2,1)S(1)} %dynamic-slice_bitcast_fusion.2), channel_id=1, source_target_pairs={{0,16},{1,17},{2,18},{3,19},{4,20},{5,21},{6,22},{7,23},{8,24},{9,... | collective-permute-start | bytes 614408 | tf_op jit(solution)/shard_map/ppermute | solution.py:246
  164.4 1.5 collective-permute-start.6
  166.0 3.0 %convolution_convert_fusion.3 = bf16[1280,40]{0,1:T(8,128)(2,1)S(1)} fusion(bf16[1280,1280]{1,0:T(8,128)(2,1)} %all-gather.3.cloned.1.call-done, s32[40]{0:T(128)S(1)} %iota_add_fusion), kind=kOutput, calls=%fused_computation.7 | convolution fusion | flops 131174400 | bytes 3379360 | tf_op jit(solution)/shard_map/dot_general | solution.py:19
  169.0 0.6 reshape.160
  169.6 0.3 reshape.161
  169.9 1.7 fusion.24
  171.8 0.6 fusion.25
  172.6 0.5 copy.64
  173.4 1.1 collective-permute-start.9
  174.6 2.3 %collective-permute-start.8 = (bf16[2,40,640]{2,1,0:T(8,128)(2,1)S(1)}, bf16[2,40,640]{2,1,0:T(8,128)(2,1)S(1)}, u32[]{:S(2)}, u32[]{:S(2)}) collective-permute-start(bf16[2,40,640]{2,1,0:T(8,128)(2,1)S(1)} %dynamic-slice_bitcast_fusion.5), channel_id=1, source_target_pairs={{0,16},{1,17},{2,18},{3,19},{4,20},{5,21},{6,22},{7,23},{8,24},{9,... | collective-permute-start | bytes 307208 | tf_op jit(solution)/shard_map/ppermute | solution.py:246
  176.9 2.4 %collective-permute-done.9 = bf16[2,40,640]{2,1,0:T(8,128)(2,1)S(1)} collective-permute-done((bf16[2,40,640]{2,1,0:T(8,128)(2,1)S(1)}, bf16[2,40,640]{2,1,0:T(8,128)(2,1)S(1)}, u32[]{:S(2)}, u32[]{:S(2)}) %collective-permute-start.9) | collective-permute-done | bytes 102432 | tf_op jit(solution)/shard_map/ppermute | solution.py:246
  179.3 2.8 %collective-permute-done.8 = bf16[2,40,640]{2,1,0:T(8,128)(2,1)S(1)} collective-permute-done((bf16[2,40,640]{2,1,0:T(8,128)(2,1)S(1)}, bf16[2,40,640]{2,1,0:T(8,128)(2,1)S(1)}, u32[]{:S(2)}, u32[]{:S(2)}) %collective-permute-start.8) | collective-permute-done | bytes 102432 | tf_op jit(solution)/shard_map/ppermute | solution.py:246
  182.2 1.3 collective-permute-done.10
  183.7 1.2 copy.61
  (62 shorter events, 3.5 us)
Async XLA Ops:
  7.2 35.1 %copy-start = (s32[64]{0:T(128)S(1)}, s32[64]{0:T(128)}, u32[]{:S(2)}) copy-start(s32[64]{0:T(128)} %param.10) | copy-start | bytes 772
  7.2 9.9 %copy-start.6 = (s32[32,2]{0,1:T(2,128)S(1)}, s32[32,2]{0,1:T(2,128)}, u32[]{:S(2)}) copy-start(s32[32,2]{0,1:T(2,128)} %param.11) | copy-start | bytes 772
  9.8 25.2 %all-to-all-start = ((bf16[2,128,1280]{2,0,1:T(2,128)(2,1)}), bf16[2,128,1280]{2,0,1:T(2,128)(2,1)S(1)}, u32[]{:S(2)}, u32[]{:S(2)}) async-start(bf16[2,128,1280]{2,0,1:T(2,128)(2,1)} %copy.47), calls=%async_computation | async-start | bytes 1310720 | tf_op jit(solution)/shard_map/all_to_all | solution.py:292
  35.3 5.7 %copy-start.5 = (f32[1280]{0:T(1024)S(1)}, f32[1280]{0:T(1024)}, u32[]{:S(2)}) copy-start(f32[1280]{0:T(1024)} %param.17) | copy-start | bytes 15364
  37.2 21.4 %all-to-all-start.1 = ((bf16[64,4,1280]{2,1,0:T(4,128)(2,1)}), bf16[64,4,1280]{2,1,0:T(4,128)(2,1)S(1)}, u32[]{:S(2)}, u32[]{:S(2)}) async-start(bf16[64,4,1280]{2,1,0:T(4,128)(2,1)} %gather_fusion), calls=%async_computation.1 | async-start | bytes 1310720 | tf_op jit(solution)/shard_map/all_to_all | solution.py:295
  40.7 125.2 %all-gather.3.cloned.1.call-start = ((), (), s32[]{:S(2)}) async-start(), calls=%async_computation.4 | async-start | bytes 3379200 | tf_op jit(solution)/shard_map/all_gather | solution.py:307
  59.9 19.9 %copy-start.1 = (bf16[256,1280]{1,0:T(8,128)(2,1)S(1)}, bf16[256,1280]{1,0:T(8,128)(2,1)}, u32[]{:S(2)}) copy-start(bf16[256,1280]{1,0:T(8,128)(2,1)} %reshape.151.x_ref) | copy-start | bytes 1966084
  79.5 7.2 %collective-permute-start.1 = (bf16[256,1280]{1,0:T(8,128)(2,1)}, bf16[256,1280]{1,0:T(8,128)(2,1)S(1)}, u32[]{:S(2)}, u32[]{:S(2)}) collective-permute-start(bf16[256,1280]{1,0:T(8,128)(2,1)} %get-tuple-element.20), channel_id=1, source_target_pairs={{0,1},{1,0},{2,3},{3,2},{4,5},{5,4},{6,7},{7,6},{8,9},{9,8},{10,11... | collective-permute-start | bytes 1966088 | tf_op jit(solution)/shard_map/ppermute | solution.py:246
  79.8 7.1 %collective-permute-start = (bf16[256,1280]{1,0:T(8,128)(2,1)S(1)}, bf16[256,1280]{1,0:T(8,128)(2,1)S(1)}, u32[]{:S(2)}, u32[]{:S(2)}) collective-permute-start(bf16[256,1280]{1,0:T(8,128)(2,1)S(1)} %copy-done.1), channel_id=1, source_target_pairs={{0,1},{1,0},{2,3},{3,2},{4,5},{5,4},{6,7},{7,6},{8,9},{9,8},{10,11... | collective-permute-start | bytes 1966088 | tf_op jit(solution)/shard_map/ppermute | solution.py:246
  82.9 3.8 %copy-start.2 = (bf16[256,1280]{1,0:T(8,128)(2,1)S(1)}, bf16[256,1280]{1,0:T(8,128)(2,1)}, u32[]{:S(2)}) copy-start(bf16[256,1280]{1,0:T(8,128)(2,1)} %get-tuple-element.19) | copy-start | bytes 1966084
  82.9 23.7 %all-to-all-start.2 = ((bf16[2,128,1280]{2,0,1:T(2,128)(2,1)}), bf16[2,128,1280]{2,0,1:T(2,128)(2,1)S(1)}, u32[]{:S(2)}, u32[]{:S(2)}) async-start(bf16[2,128,1280]{2,0,1:T(2,128)(2,1)} %copy.55), calls=%async_computation.2 | async-start | bytes 1310720 | tf_op jit(solution)/shard_map/all_to_all | solution.py:309
  86.8 1.3 copy-start.4
  86.9 1.4 copy-start.3
  89.4 46.8 %collective-permute-start.3 = (bf16[2,2,2,2,40,640]{5,4,3,1,0,2:T(8,128)(2,1)}, bf16[2,2,2,2,40,640]{5,4,3,1,0,2:T(8,128)(2,1)}, u32[]{:S(2)}, u32[]{:S(2)}) collective-permute-start(bf16[2,2,2,2,40,640]{5,4,3,1,0,2:T(8,128)(2,1)} %bitcast.99), channel_id=1, source_target_pairs={{0,4},{1,5},{2,6},{3,7},{4,0},{5,1},{6,2},{7,3},{8,12},{9,13},{10,... | collective-permute-start | bytes 2457608 | tf_op jit(solution)/shard_map/ppermute | solution.py:246
  108.6 27.2 %all-to-all-start.3 = ((bf16[64,4,1280]{2,1,0:T(4,128)(2,1)}), bf16[64,4,1280]{2,1,0:T(4,128)(2,1)S(1)}, u32[]{:S(2)}, u32[]{:S(2)}) async-start(bf16[64,4,1280]{2,1,0:T(4,128)(2,1)} %reshape.158), calls=%async_computation.3 | async-start | bytes 1310720 | tf_op jit(solution)/shard_map/all_to_all | solution.py:335
  115.9 31.1 %collective-permute-start.2 = (bf16[2,2,2,2,40,640]{5,4,3,0,1,2:T(8,128)(2,1)}, bf16[2,2,2,2,40,640]{5,4,3,0,1,2:T(8,128)(2,1)}, u32[]{:S(2)}, u32[]{:S(2)}) collective-permute-start(bf16[2,2,2,2,40,640]{5,4,3,0,1,2:T(8,128)(2,1)} %bitcast.100), channel_id=1, source_target_pairs={{0,2},{1,3},{2,0},{3,1},{4,6},{5,7},{6,4},{7,5},{8,10},{9,11},{10,... | collective-permute-start | bytes 2457608 | tf_op jit(solution)/shard_map/ppermute | solution.py:246
  148.4 11.3 %collective-permute-start.5 = (bf16[2,2,2,40,640]{4,3,2,1,0:T(8,128)(2,1)S(1)}, bf16[2,2,2,40,640]{4,3,2,1,0:T(8,128)(2,1)S(1)}, u32[]{:S(2)}, u32[]{:S(2)}) collective-permute-start(bf16[2,2,2,40,640]{4,3,2,1,0:T(8,128)(2,1)S(1)} %dynamic-slice_bitcast_fusion), channel_id=1, source_target_pairs={{0,2},{1,3},{2,0},{3,1},{4,6},{5,7},{6,4},{7,5},{8,10},{9,11},{10,... | collective-permute-start | bytes 1228808 | tf_op jit(solution)/shard_map/ppermute | solution.py:246
  150.9 10.7 %collective-permute-start.4 = (bf16[2,2,2,40,640]{4,3,2,0,1:T(8,128)(2,1)S(1)}, bf16[2,2,2,40,640]{4,3,2,0,1:T(8,128)(2,1)S(1)}, u32[]{:S(2)}, u32[]{:S(2)}) collective-permute-start(bf16[2,2,2,40,640]{4,3,2,0,1:T(8,128)(2,1)S(1)} %dynamic-slice_bitcast_fusion.1), channel_id=1, source_target_pairs={{0,4},{1,5},{2,6},{3,7},{4,0},{5,1},{6,2},{7,3},{8,12},{9,13},{10,... | collective-permute-start | bytes 1228808 | tf_op jit(solution)/shard_map/ppermute | solution.py:246
  161.8 11.5 %collective-permute-start.7 = (bf16[2,2,40,640]{3,2,1,0:T(8,128)(2,1)S(1)}, bf16[2,2,40,640]{3,2,1,0:T(8,128)(2,1)S(1)}, u32[]{:S(2)}, u32[]{:S(2)}) collective-permute-start(bf16[2,2,40,640]{3,2,1,0:T(8,128)(2,1)S(1)} %dynamic-slice_bitcast_fusion.2), channel_id=1, source_target_pairs={{0,16},{1,17},{2,18},{3,19},{4,20},{5,21},{6,22},{7,23},{8,24},{9,... | collective-permute-start | bytes 614408 | tf_op jit(solution)/shard_map/ppermute | solution.py:246
  164.4 8.8 %collective-permute-start.6 = (bf16[2,2,40,640]{3,2,1,0:T(8,128)(2,1)S(1)}, bf16[2,2,40,640]{3,2,1,0:T(8,128)(2,1)S(1)}, u32[]{:S(2)}, u32[]{:S(2)}) collective-permute-start(bf16[2,2,40,640]{3,2,1,0:T(8,128)(2,1)S(1)} %dynamic-slice_bitcast_fusion.3), channel_id=1, source_target_pairs={{0,8},{1,9},{2,10},{3,11},{4,12},{5,13},{6,14},{7,15},{8,0},{9,1},... | collective-permute-start | bytes 614408 | tf_op jit(solution)/shard_map/ppermute | solution.py:246
  173.4 5.9 %collective-permute-start.9 = (bf16[2,40,640]{2,1,0:T(8,128)(2,1)S(1)}, bf16[2,40,640]{2,1,0:T(8,128)(2,1)S(1)}, u32[]{:S(2)}, u32[]{:S(2)}) collective-permute-start(bf16[2,40,640]{2,1,0:T(8,128)(2,1)S(1)} %dynamic-slice_bitcast_fusion.4), channel_id=1, source_target_pairs={{0,8},{1,9},{2,10},{3,11},{4,12},{5,13},{6,14},{7,15},{8,0},{9,1},... | collective-permute-start | bytes 307208 | tf_op jit(solution)/shard_map/ppermute | solution.py:246
  174.6 7.5 %collective-permute-start.8 = (bf16[2,40,640]{2,1,0:T(8,128)(2,1)S(1)}, bf16[2,40,640]{2,1,0:T(8,128)(2,1)S(1)}, u32[]{:S(2)}, u32[]{:S(2)}) collective-permute-start(bf16[2,40,640]{2,1,0:T(8,128)(2,1)S(1)} %dynamic-slice_bitcast_fusion.5), channel_id=1, source_target_pairs={{0,16},{1,17},{2,18},{3,19},{4,20},{5,21},{6,22},{7,23},{8,24},{9,... | collective-permute-start | bytes 307208 | tf_op jit(solution)/shard_map/ppermute | solution.py:246
  182.2 1.4 collective-permute-start.10
Sparse Core Ops, SparseCore 0:
  79.6 68.3 all-gather.2

commit v5 on v4

--- a/solution.py
+++ b/solution.py
@@ -335,14 +335,12 @@
             d_embeddings = lax.all_to_all(
                 summed, "dev", split_axis=0, concat_axis=1, tiled=True
             )
+            came = list(lax.optimization_barrier(tuple(came)))
+        elif turn == 1:
             came[0], came[1], d_embeddings = lax.optimization_barrier(
                 (came[0], came[1], d_embeddings)
             )
             d_embeddings = d_embeddings.astype(F32)
-        elif turn == 1:
-            came[0], came[1], d_embeddings = lax.optimization_barrier(
-                (came[0], came[1], d_embeddings)
-            )
             small_grads = factor_grads(factors, me, n)
         elif turn == 2:
             came[0], came[1], d_embeddings, small_grads = lax.optimization_barrier(

time: 192 us -> 177 us (0.922)
  waiting for transfers between devices: 92.3 us -> 79.5 us
  starting transfers between devices: 31.8 us -> 27.1 us
  local copies, waits for them, and re-layouts: 20.2 us -> 22.5 us
    all_to_all x1, waiting for transfers between devices: 18.2 us -> 5.44 us  [shards(): lax.all_to_all(summed, 'dev', split_axis=0, concat_axis=1, tiled=True)]
    all_to_all x1, waiting for transfers between devices: 15.6 us -> 10.7 us  [shards(): lax.all_to_all(slot_grads, 'dev', split_axis=1, concat_axis=0, tiled=True)]
    ppermute x11, waiting for transfers between devices: 25.7 us -> 30.4 us  [swap(): return lax.ppermute(value, 'dev', [(i, i ^ 1 << bit) for i in range(n)])]
    ppermute x11, starting transfers between devices: 13.8 us -> 9.08 us  [swap(): return lax.ppermute(value, 'dev', [(i, i ^ 1 << bit) for i in range(n)])]
    unnamed x21 -> x19, local copies, waits for them, and re-layouts: 4.73 us -> 4.56 us
  transfers between devices with their start and end apart: 16 -> 16, of which waited for: 10 -> 12; matrix products, arithmetic and copies ran while one was open for 13% -> 16% of each run, Pallas kernels for 0% -> 0%
where the time goes in v5:
time: 177 us
  waiting for transfers between devices  79.5 us (45%)
  starting transfers between devices  27.1 us (15%)
  local copies, waits for them, and re-layouts  22.5 us (13%)
  Pallas kernels  19.6 us (11%)
  between operations  15.1 us (9%)
  matrix products  6.53 us (4%)
  other arithmetic  6.19 us (3%)
    ppermute x11, waiting for transfers between devices, swap(): return lax.ppermute(value, 'dev', [(i, i ^ 1 << bit) for i in range(n)])  30.4 us
    pallas_call x1, Pallas kernels, local_step(): pl.pallas_call(local_kernel, out_shape=(like, like, like, jax.ShapeDtypeS...  19.6 us
    all_to_all x1, waiting for transfers between devices, shards(): lax.all_to_all(embeddings, 'dev', split_axis=1, concat_axis=0, tiled=True)  17.7 us
    all_to_all x1, waiting for transfers between devices, shards(): lax.all_to_all(picked, 'dev', split_axis=0, concat_axis=1, tiled=True)  15.2 us
    all_to_all x1, waiting for transfers between devices, shards(): lax.all_to_all(slot_grads, 'dev', split_axis=1, concat_axis=0, tiled=True)  10.7 us
    ppermute x11, starting transfers between devices, swap(): return lax.ppermute(value, 'dev', [(i, i ^ 1 << bit) for i in range(n)])  9.08 us
    all_to_all x1, starting transfers between devices, shards(): lax.all_to_all(embeddings, 'dev', split_axis=1, concat_axis=0, tiled=True)  7.3 us
    dot_general x6, matrix products, mm(): return lax.dot_general(a, b, dims, preferred_element_type=F32)  6.53 us
  transfers between devices with their start and end apart: 16, of which 12 were waited for; matrix products, arithmetic and copies ran while one was open for 16% of the time, Pallas kernels for 0%

profile of v5, /device:TPU:0, one launch (start us, length us, event | category | flops | bytes accessed | tf_op | source)
XLA Modules:
  0.0 176.7 jit_solution(15493189167664553141)
XLA Ops:
  7.2 2.6 %copy.47 = bf16[2,128,1280]{2,0,1:T(2,128)(2,1)} copy(bf16[2,128,1280]{2,1,0:T(8,128)(2,1)} %param.9) | data formatting | bytes 1310720 | tf_op args[0]
  9.8 7.3 %all-to-all-start = ((bf16[2,128,1280]{2,0,1:T(2,128)(2,1)}), bf16[2,128,1280]{2,0,1:T(2,128)(2,1)S(1)}, u32[]{:S(2)}, u32[]{:S(2)}) async-start(bf16[2,128,1280]{2,0,1:T(2,128)(2,1)} %copy.47), calls=%async_computation | async-start | bytes 1310720 | tf_op jit(solution)/shard_map/all_to_all | solution.py:292
  17.3 17.7 %all-to-all-done = bf16[2,128,1280]{2,0,1:T(2,128)(2,1)S(1)} async-done(((bf16[2,128,1280]{2,0,1:T(2,128)(2,1)}), bf16[2,128,1280]{2,0,1:T(2,128)(2,1)S(1)}, u32[]{:S(2)}, u32[]{:S(2)}) %all-to-all-start) | async-done | bytes 655392 | tf_op jit(solution)/shard_map/all_to_all | solution.py:292
  35.3 1.9 %gather_fusion = bf16[64,4,1280]{2,1,0:T(4,128)(2,1)} fusion(bf16[64,4,1280]{2,1,0:T(4,128)(2,1)S(1)} %bitcast.110, s32[1024]{0:T(1024)S(1)} %pad_clamp_fusion.1), kind=kCustom, calls=%fused_computation | custom fusion | bytes 1310976 | tf_op jit(solution)/shard_map/gather | solution.py:294
  37.2 3.5 %all-to-all-start.1 = ((bf16[64,4,1280]{2,1,0:T(4,128)(2,1)}), bf16[64,4,1280]{2,1,0:T(4,128)(2,1)S(1)}, u32[]{:S(2)}, u32[]{:S(2)}) async-start(bf16[64,4,1280]{2,1,0:T(4,128)(2,1)} %gather_fusion), calls=%async_computation.1 | async-start | bytes 1310720 | tf_op jit(solution)/shard_map/all_to_all | solution.py:295
  41.0 0.6 reshape.153.wc_ref
  42.2 1.2 gather_fusion.1
  43.4 15.2 %all-to-all-done.1 = bf16[64,4,1280]{2,1,0:T(4,128)(2,1)S(1)} async-done(((bf16[64,4,1280]{2,1,0:T(4,128)(2,1)}), bf16[64,4,1280]{2,1,0:T(4,128)(2,1)S(1)}, u32[]{:S(2)}, u32[]{:S(2)}) %all-to-all-start.1) | async-done | bytes 655392 | tf_op jit(solution)/shard_map/all_to_all | solution.py:295
  58.9 1.0 reshape.151.x_ref
  59.9 19.6 %shard_map.104 = (bf16[256,1280]{1,0:T(8,128)(2,1)}, bf16[256,1280]{1,0:T(8,128)(2,1)}, bf16[256,1280]{1,0:T(8,128)(2,1)}, bf16[40,1280]{1,0:T(8,128)(2,1)}) custom-call(s32[2]{0:T(128)} %gather_fusion.1, s32[1]{0:T(128)S(6)} %copy.83.label_ref, s32[1]{0:T(128)} %bitcast.7.core_ref, bf16[256,1280]{1,0:T(8,128)(2,1)} %reshape.151.x_ref, ...), custom_call_target="tpu_custom_call" | custom-call | flops 5033164800 | bytes 18350080 | tf_op jit(solution)/shard_map/pallas_call | solution.py:213
  79.7 0.4 collective-permute-start
  80.1 2.6 %copy.56 = bf16[2,128,1280]{2,0,1:T(2,128)(2,1)} copy(bf16[2,128,1280]{2,1,0:T(8,128)(2,1)} %bitcast.118) | data formatting | bytes 1310720 | tf_op jit(solution)/shard_map/reshape | solution.py:308
  82.7 3.7 %all-to-all-start.2 = ((bf16[2,128,1280]{2,0,1:T(2,128)(2,1)}), bf16[2,128,1280]{2,0,1:T(2,128)(2,1)S(1)}, u32[]{:S(2)}, u32[]{:S(2)}) async-start(bf16[2,128,1280]{2,0,1:T(2,128)(2,1)} %copy.56), calls=%async_computation.2 | async-start | bytes 1310720 | tf_op jit(solution)/shard_map/all_to_all | solution.py:309
  86.6 1.1 constant_dynamic-update-slice_fusion
  87.8 1.2 convolution_convert_fusion.1
  89.1 1.0 copy.78
  90.1 1.6 collective-permute-start.3
  91.7 1.2 convolution_convert_fusion.2
  93.1 1.0 copy.79
  94.1 1.5 collective-permute-start.2
  95.6 10.7 %all-to-all-done.2 = bf16[2,128,1280]{2,0,1:T(2,128)(2,1)S(1)} async-done(((bf16[2,128,1280]{2,0,1:T(2,128)(2,1)}), bf16[2,128,1280]{2,0,1:T(2,128)(2,1)S(1)}, u32[]{:S(2)}, u32[]{:S(2)}) %all-to-all-start.2) | async-done | bytes 655392 | tf_op jit(solution)/shard_map/all_to_all | solution.py:309
  107.0 1.3 reshape.158
  108.3 3.5 %all-to-all-start.3 = ((bf16[64,4,1280]{2,1,0:T(4,128)(2,1)}), bf16[64,4,1280]{2,1,0:T(4,128)(2,1)S(1)}, u32[]{:S(2)}, u32[]{:S(2)}) async-start(bf16[64,4,1280]{2,1,0:T(4,128)(2,1)} %reshape.158), calls=%async_computation.3 | async-start | bytes 1310720 | tf_op jit(solution)/shard_map/all_to_all | solution.py:335
  111.8 0.5 iota_add_fusion
  112.4 5.0 %collective-permute-done.3 = bf16[2,2,2,2,40,640]{5,4,3,1,0,2:T(8,128)(2,1)} collective-permute-done((bf16[2,2,2,2,40,640]{5,4,3,1,0,2:T(8,128)(2,1)}, bf16[2,2,2,2,40,640]{5,4,3,1,0,2:T(8,128)(2,1)}, u32[]{:S(2)}, u32[]{:S(2)}) %collective-permute-start.3) | collective-permute-done | bytes 819232 | tf_op jit(solution)/shard_map/ppermute | solution.py:246
  117.4 5.7 %collective-permute-done.2 = bf16[2,2,2,2,40,640]{5,4,3,0,1,2:T(8,128)(2,1)} collective-permute-done((bf16[2,2,2,2,40,640]{5,4,3,0,1,2:T(8,128)(2,1)}, bf16[2,2,2,2,40,640]{5,4,3,0,1,2:T(8,128)(2,1)}, u32[]{:S(2)}, u32[]{:S(2)}) %collective-permute-start.2) | collective-permute-done | bytes 819232 | tf_op jit(solution)/shard_map/ppermute | solution.py:246
  123.1 1.3 fusion
  124.4 0.8 dynamic-slice_bitcast_fusion
  125.2 1.9 %collective-permute-start.5 = (bf16[2,2,2,40,640]{4,3,2,1,0:T(8,128)(2,1)}, bf16[2,2,2,40,640]{4,3,2,1,0:T(8,128)(2,1)}, u32[]{:S(2)}, u32[]{:S(2)}) collective-permute-start(bf16[2,2,2,40,640]{4,3,2,1,0:T(8,128)(2,1)} %dynamic-slice_bitcast_fusion), channel_id=1, source_target_pairs={{0,2},{1,3},{2,0},{3,1},{4,6},{5,7},{6,4},{7,5},{8,10},{9,11},{10,... | collective-permute-start | bytes 1228808 | tf_op jit(solution)/shard_map/ppermute | solution.py:246
  127.1 1.4 fusion.1
  128.5 0.8 dynamic-slice_bitcast_fusion.1
  129.3 0.7 collective-permute-start.4
  130.0 5.4 %all-to-all-done.3 = bf16[64,4,1280]{2,1,0:T(4,128)(2,1)S(1)} async-done(((bf16[64,4,1280]{2,1,0:T(4,128)(2,1)}), bf16[64,4,1280]{2,1,0:T(4,128)(2,1)S(1)}, u32[]{:S(2)}, u32[]{:S(2)}) %all-to-all-start.3) | async-done | bytes 655392 | tf_op jit(solution)/shard_map/all_to_all | solution.py:335
  135.8 6.3 %collective-permute-done.5 = bf16[2,2,2,40,640]{4,3,2,1,0:T(8,128)(2,1)} collective-permute-done((bf16[2,2,2,40,640]{4,3,2,1,0:T(8,128)(2,1)}, bf16[2,2,2,40,640]{4,3,2,1,0:T(8,128)(2,1)}, u32[]{:S(2)}, u32[]{:S(2)}) %collective-permute-start.5) | collective-permute-done | bytes 409632 | tf_op jit(solution)/shard_map/ppermute | solution.py:246
  142.0 2.4 %collective-permute-done.4 = bf16[2,2,2,40,640]{4,3,2,0,1:T(8,128)(2,1)S(1)} collective-permute-done((bf16[2,2,2,40,640]{4,3,2,0,1:T(8,128)(2,1)}, bf16[2,2,2,40,640]{4,3,2,0,1:T(8,128)(2,1)S(1)}, u32[]{:S(2)}, u32[]{:S(2)}) %collective-permute-start.4) | collective-permute-done | bytes 409632 | tf_op jit(solution)/shard_map/ppermute | solution.py:246
  144.4 1.1 fusion.2
  145.6 2.6 %collective-permute-start.7 = (bf16[2,2,40,640]{3,2,1,0:T(8,128)(2,1)S(1)}, bf16[2,2,40,640]{3,2,1,0:T(8,128)(2,1)S(1)}, u32[]{:S(2)}, u32[]{:S(2)}) collective-permute-start(bf16[2,2,40,640]{3,2,1,0:T(8,128)(2,1)S(1)} %dynamic-slice_bitcast_fusion.2), channel_id=1, source_target_pairs={{0,16},{1,17},{2,18},{3,19},{4,20},{5,21},{6,22},{7,23},{8,24},{9,... | collective-permute-start | bytes 614408 | tf_op jit(solution)/shard_map/ppermute | solution.py:246
  148.2 1.1 convert_element_type.135
  149.6 3.0 %convolution_convert_fusion.3 = bf16[1280,40]{0,1:T(8,128)(2,1)S(1)} fusion(bf16[1280,1280]{1,0:T(8,128)(2,1)} %all-gather.3.cloned.1.call-done, s32[40]{0:T(128)S(1)} %copy-done.5), kind=kOutput, calls=%fused_computation.7 | convolution fusion | flops 131174400 | bytes 3379360 | tf_op jit(solution)/shard_map/dot_general | solution.py:19
  152.6 0.6 reshape.160
  153.5 1.7 fusion.24
  155.5 0.6 fusion.25
  156.2 0.5 copy.64
  156.9 2.7 %collective-permute-done.6 = bf16[2,2,40,640]{3,2,1,0:T(8,128)(2,1)S(1)} collective-permute-done((bf16[2,2,40,640]{3,2,1,0:T(8,128)(2,1)S(1)}, bf16[2,2,40,640]{3,2,1,0:T(8,128)(2,1)S(1)}, u32[]{:S(2)}, u32[]{:S(2)}) %collective-permute-start.6) | collective-permute-done | bytes 204832 | tf_op jit(solution)/shard_map/ppermute | solution.py:246
  159.9 4.9 %collective-permute-done.9 = bf16[2,40,640]{2,1,0:T(8,128)(2,1)S(1)} collective-permute-done((bf16[2,40,640]{2,1,0:T(8,128)(2,1)S(1)}, bf16[2,40,640]{2,1,0:T(8,128)(2,1)S(1)}, u32[]{:S(2)}, u32[]{:S(2)}) %collective-permute-start.9) | collective-permute-done | bytes 102432 | tf_op jit(solution)/shard_map/ppermute | solution.py:246
  164.8 2.2 %collective-permute-done.8 = bf16[2,40,640]{2,1,0:T(8,128)(2,1)S(1)} collective-permute-done((bf16[2,40,640]{2,1,0:T(8,128)(2,1)S(1)}, bf16[2,40,640]{2,1,0:T(8,128)(2,1)S(1)}, u32[]{:S(2)}, u32[]{:S(2)}) %collective-permute-start.8) | collective-permute-done | bytes 102432 | tf_op jit(solution)/shard_map/ppermute | solution.py:246
  167.2 1.3 collective-permute-done.10
  168.6 1.2 copy.61
  (60 shorter events, 4.4 us)
Async XLA Ops:
  7.2 35.1 %copy-start = (s32[64]{0:T(128)S(1)}, s32[64]{0:T(128)}, u32[]{:S(2)}) copy-start(s32[64]{0:T(128)} %param.10) | copy-start | bytes 772
  7.2 9.9 %copy-start.4 = (s32[32,2]{0,1:T(2,128)S(1)}, s32[32,2]{0,1:T(2,128)}, u32[]{:S(2)}) copy-start(s32[32,2]{0,1:T(2,128)} %param.11) | copy-start | bytes 772
  9.8 25.2 %all-to-all-start = ((bf16[2,128,1280]{2,0,1:T(2,128)(2,1)}), bf16[2,128,1280]{2,0,1:T(2,128)(2,1)S(1)}, u32[]{:S(2)}, u32[]{:S(2)}) async-start(bf16[2,128,1280]{2,0,1:T(2,128)(2,1)} %copy.47), calls=%async_computation | async-start | bytes 1310720 | tf_op jit(solution)/shard_map/all_to_all | solution.py:292
  35.3 5.7 %copy-start.3 = (f32[1280]{0:T(1024)S(1)}, f32[1280]{0:T(1024)}, u32[]{:S(2)}) copy-start(f32[1280]{0:T(1024)} %param.17) | copy-start | bytes 15364
  37.2 21.4 %all-to-all-start.1 = ((bf16[64,4,1280]{2,1,0:T(4,128)(2,1)}), bf16[64,4,1280]{2,1,0:T(4,128)(2,1)S(1)}, u32[]{:S(2)}, u32[]{:S(2)}) async-start(bf16[64,4,1280]{2,1,0:T(4,128)(2,1)} %gather_fusion), calls=%async_computation.1 | async-start | bytes 1310720 | tf_op jit(solution)/shard_map/all_to_all | solution.py:295
  40.7 108.9 %all-gather.3.cloned.1.call-start = ((), (), s32[]{:S(2)}) async-start(), calls=%async_computation.4 | async-start | bytes 3379200 | tf_op jit(solution)/shard_map/all_gather | solution.py:307
  59.9 19.8 %copy-start.1 = (bf16[256,1280]{1,0:T(8,128)(2,1)S(1)}, bf16[256,1280]{1,0:T(8,128)(2,1)}, u32[]{:S(2)}) copy-start(bf16[256,1280]{1,0:T(8,128)(2,1)} %reshape.151.x_ref) | copy-start | bytes 1966084
  79.5 7.0 %collective-permute-start.1 = (bf16[256,1280]{1,0:T(8,128)(2,1)}, bf16[256,1280]{1,0:T(8,128)(2,1)S(1)}, u32[]{:S(2)}, u32[]{:S(2)}) collective-permute-start(bf16[256,1280]{1,0:T(8,128)(2,1)} %get-tuple-element.19), channel_id=1, source_target_pairs={{0,1},{1,0},{2,3},{3,2},{4,5},{5,4},{6,7},{7,6},{8,9},{9,8},{10,11... | collective-permute-start | bytes 1966088 | tf_op jit(solution)/shard_map/ppermute | solution.py:246
  79.7 7.0 %collective-permute-start = (bf16[256,1280]{1,0:T(8,128)(2,1)S(1)}, bf16[256,1280]{1,0:T(8,128)(2,1)}, u32[]{:S(2)}, u32[]{:S(2)}) collective-permute-start(bf16[256,1280]{1,0:T(8,128)(2,1)S(1)} %copy-done.1), channel_id=1, source_target_pairs={{0,1},{1,0},{2,3},{3,2},{4,5},{5,4},{6,7},{7,6},{8,9},{9,8},{10,11... | collective-permute-start | bytes 1966088 | tf_op jit(solution)/shard_map/ppermute | solution.py:246
  82.7 3.8 %copy-start.2 = (bf16[256,1280]{1,0:T(8,128)(2,1)S(1)}, bf16[256,1280]{1,0:T(8,128)(2,1)}, u32[]{:S(2)}) copy-start(bf16[256,1280]{1,0:T(8,128)(2,1)} %get-tuple-element.18) | copy-start | bytes 1966084
  82.7 23.7 %all-to-all-start.2 = ((bf16[2,128,1280]{2,0,1:T(2,128)(2,1)}), bf16[2,128,1280]{2,0,1:T(2,128)(2,1)S(1)}, u32[]{:S(2)}, u32[]{:S(2)}) async-start(bf16[2,128,1280]{2,0,1:T(2,128)(2,1)} %copy.56), calls=%async_computation.2 | async-start | bytes 1310720 | tf_op jit(solution)/shard_map/all_to_all | solution.py:309
  90.1 27.3 %collective-permute-start.3 = (bf16[2,2,2,2,40,640]{5,4,3,1,0,2:T(8,128)(2,1)}, bf16[2,2,2,2,40,640]{5,4,3,1,0,2:T(8,128)(2,1)}, u32[]{:S(2)}, u32[]{:S(2)}) collective-permute-start(bf16[2,2,2,2,40,640]{5,4,3,1,0,2:T(8,128)(2,1)} %bitcast.99), channel_id=1, source_target_pairs={{0,4},{1,5},{2,6},{3,7},{4,0},{5,1},{6,2},{7,3},{8,12},{9,13},{10,... | collective-permute-start | bytes 2457608 | tf_op jit(solution)/shard_map/ppermute | solution.py:246
  94.1 29.0 %collective-permute-start.2 = (bf16[2,2,2,2,40,640]{5,4,3,0,1,2:T(8,128)(2,1)}, bf16[2,2,2,2,40,640]{5,4,3,0,1,2:T(8,128)(2,1)}, u32[]{:S(2)}, u32[]{:S(2)}) collective-permute-start(bf16[2,2,2,2,40,640]{5,4,3,0,1,2:T(8,128)(2,1)} %bitcast.100), channel_id=1, source_target_pairs={{0,2},{1,3},{2,0},{3,1},{4,6},{5,7},{6,4},{7,5},{8,10},{9,11},{10,... | collective-permute-start | bytes 2457608 | tf_op jit(solution)/shard_map/ppermute | solution.py:246
  108.3 27.1 %all-to-all-start.3 = ((bf16[64,4,1280]{2,1,0:T(4,128)(2,1)}), bf16[64,4,1280]{2,1,0:T(4,128)(2,1)S(1)}, u32[]{:S(2)}, u32[]{:S(2)}) async-start(bf16[64,4,1280]{2,1,0:T(4,128)(2,1)} %reshape.158), calls=%async_computation.3 | async-start | bytes 1310720 | tf_op jit(solution)/shard_map/all_to_all | solution.py:335
  125.2 16.8 %collective-permute-start.5 = (bf16[2,2,2,40,640]{4,3,2,1,0:T(8,128)(2,1)}, bf16[2,2,2,40,640]{4,3,2,1,0:T(8,128)(2,1)}, u32[]{:S(2)}, u32[]{:S(2)}) collective-permute-start(bf16[2,2,2,40,640]{4,3,2,1,0:T(8,128)(2,1)} %dynamic-slice_bitcast_fusion), channel_id=1, source_target_pairs={{0,2},{1,3},{2,0},{3,1},{4,6},{5,7},{6,4},{7,5},{8,10},{9,11},{10,... | collective-permute-start | bytes 1228808 | tf_op jit(solution)/shard_map/ppermute | solution.py:246
  129.3 15.1 %collective-permute-start.4 = (bf16[2,2,2,40,640]{4,3,2,0,1:T(8,128)(2,1)}, bf16[2,2,2,40,640]{4,3,2,0,1:T(8,128)(2,1)S(1)}, u32[]{:S(2)}, u32[]{:S(2)}) collective-permute-start(bf16[2,2,2,40,640]{4,3,2,0,1:T(8,128)(2,1)} %dynamic-slice_bitcast_fusion.1), channel_id=1, source_target_pairs={{0,4},{1,5},{2,6},{3,7},{4,0},{5,1},{6,2},{7,3},{8,12},{9,13},{10,... | collective-permute-start | bytes 1228808 | tf_op jit(solution)/shard_map/ppermute | solution.py:246
  145.6 4.0 %copy-start.5 = (s32[40]{0:T(128)S(1)}, s32[40]{0:T(128)}, u32[]{:S(2)}) copy-start(s32[40]{0:T(128)} %iota_add_fusion) | copy-start | bytes 484
  145.6 11.3 %collective-permute-start.7 = (bf16[2,2,40,640]{3,2,1,0:T(8,128)(2,1)S(1)}, bf16[2,2,40,640]{3,2,1,0:T(8,128)(2,1)S(1)}, u32[]{:S(2)}, u32[]{:S(2)}) collective-permute-start(bf16[2,2,40,640]{3,2,1,0:T(8,128)(2,1)S(1)} %dynamic-slice_bitcast_fusion.2), channel_id=1, source_target_pairs={{0,16},{1,17},{2,18},{3,19},{4,20},{5,21},{6,22},{7,23},{8,24},{9,... | collective-permute-start | bytes 614408 | tf_op jit(solution)/shard_map/ppermute | solution.py:246
  149.5 10.1 %collective-permute-start.6 = (bf16[2,2,40,640]{3,2,1,0:T(8,128)(2,1)S(1)}, bf16[2,2,40,640]{3,2,1,0:T(8,128)(2,1)S(1)}, u32[]{:S(2)}, u32[]{:S(2)}) collective-permute-start(bf16[2,2,40,640]{3,2,1,0:T(8,128)(2,1)S(1)} %dynamic-slice_bitcast_fusion.3), channel_id=1, source_target_pairs={{0,8},{1,9},{2,10},{3,11},{4,12},{5,13},{6,14},{7,15},{8,0},{9,1},... | collective-permute-start | bytes 614408 | tf_op jit(solution)/shard_map/ppermute | solution.py:246
  159.7 5.2 %collective-permute-start.9 = (bf16[2,40,640]{2,1,0:T(8,128)(2,1)S(1)}, bf16[2,40,640]{2,1,0:T(8,128)(2,1)S(1)}, u32[]{:S(2)}, u32[]{:S(2)}) collective-permute-start(bf16[2,40,640]{2,1,0:T(8,128)(2,1)S(1)} %dynamic-slice_bitcast_fusion.4), channel_id=1, source_target_pairs={{0,8},{1,9},{2,10},{3,11},{4,12},{5,13},{6,14},{7,15},{8,0},{9,1},... | collective-permute-start | bytes 307208 | tf_op jit(solution)/shard_map/ppermute | solution.py:246
  159.9 7.2 %collective-permute-start.8 = (bf16[2,40,640]{2,1,0:T(8,128)(2,1)S(1)}, bf16[2,40,640]{2,1,0:T(8,128)(2,1)S(1)}, u32[]{:S(2)}, u32[]{:S(2)}) collective-permute-start(bf16[2,40,640]{2,1,0:T(8,128)(2,1)S(1)} %dynamic-slice_bitcast_fusion.5), channel_id=1, source_target_pairs={{0,16},{1,17},{2,18},{3,19},{4,20},{5,21},{6,22},{7,23},{8,24},{9,... | collective-permute-start | bytes 307208 | tf_op jit(solution)/shard_map/ppermute | solution.py:246
  167.1 1.4 collective-permute-start.10
Sparse Core Ops, SparseCore 0:
  79.6 69.9 all-gather.2
